TPU v7x, 32 devices: a whole 2x2x4 slice. The times are simulated.
32 devices in a mesh: replica: 8 (over y, x, core), fsdp: 4 (over z).
Axes of the slice: x: 2, y: 2, z: 4, core: 2. Of those that a mesh axis runs over, the one named last changes fastest.
Arguments:
- hidden: bfloat16 [8, 2, 256, 8192], P('replica', None, 'fsdp'), may hold values from -6 to 6
- targets: bfloat16 [8, 2, 256, 512], P('replica', None, 'fsdp'), may hold values from -16 to 16
- doc_ids: int32 [8, 2, 256], P('replica', None, 'fsdp'), may hold values from 0 to 7, never falling along the last dimension, each value on 1 to 64 neighbouring positions
- weights: bfloat16 [8, 8192, 512], P('replica', 'fsdp'), may hold values from -5 to 5
- adam_m: bfloat16 [8, 8192, 512], P('replica', 'fsdp'), may hold values from -1.335144e-05 to 1.335144e-05
- adam_v: bfloat16 [8, 8192, 512], P('replica', 'fsdp'), may hold values from 3.623768e-13 to 3.6379788e-11
- anchor: bfloat16 [8192, 128], P('fsdp'), may hold values from -5 to 5
- momentum: bfloat16 [8192, 128], P('fsdp'), may hold values from -5 to 5
- fragment: int32 [1], replicated, may hold values from 0 to 3
Outputs:
- new_weights: float32 [8, 8192, 512], P('replica', 'fsdp')
- losses: float32 [8, 2], P('replica')
Inputs may be any that keep to these rules, and one draw needn't show every extreme that they name: `doc_ids`: in each row (replica, step) the document numbers never fall, every number 0 to 7 occurs, each document has 1 to 64 tokens and one has exactly 64.
All inputs are finite; a program needn't handle non-finite values.
Results may differ from a plain program's by a relative error of at most 0.0003.
Values may be sent and summed in bfloat16 or wider, within the bound.
A program may use at most 64 MiB of HBM per device.

v0:
```python
import jax
import jax.numpy as jnp
from jax import lax
from jax.sharding import PartitionSpec as P

DOCS = 8


NORM_EPS = 1e-05
ADAM_EPS = 1e-08
INNER_RATE = 0.1
DECAY_RATE = 0.1
BETA_FIRST = 0.9
BETA_SECOND = 0.95
OUTER_RATE = 0.7
NESTEROV = 0.9
MIXING = 0.5


def normalize(block):
    wide = block.astype(jnp.float32)
    power = jnp.mean(wide * wide, axis=-1, keepdims=True)
    return (wide * lax.rsqrt(power + NORM_EPS)).astype(jnp.bfloat16)


def outer_update(anchor_rows, moment_rows, mean_delta):
    new_moment = NESTEROV * moment_rows + mean_delta
    return anchor_rows - OUTER_RATE * (mean_delta + NESTEROV * new_moment)


def adam_update(master, first, second, gradient):
    first = BETA_FIRST * first + (1.0 - BETA_FIRST) * gradient
    second = BETA_SECOND * second + (1.0 - BETA_SECOND) * gradient * gradient
    master = master - INNER_RATE * (first / (jnp.sqrt(second) + ADAM_EPS) + DECAY_RATE * master)
    return (master, first, second)


def body(hidden, targets, doc_ids, weights, adam_m, adam_v, anchor, momentum, fragment):
    steps_total = hidden.shape[1]
    model_width = hidden.shape[3]
    value_width = weights.shape[2]
    shard_rows = weights.shape[1]
    frag_width = anchor.shape[1]
    scale = model_width ** (-0.5)
    zero = jnp.zeros((), jnp.int32)
    start = fragment[0] * frag_width
    local = lax.dynamic_slice(weights[0], (zero, start), (shard_rows, frag_width))
    delta = anchor.astype(jnp.float32) - local.astype(jnp.float32)
    replicas = lax.axis_size("replica")
    mean_delta = lax.psum(delta, "replica") / replicas
    global_fragment = outer_update(
        anchor.astype(jnp.float32), momentum.astype(jnp.float32), mean_delta
    )
    doc_range = jnp.arange(DOCS, dtype=jnp.int32)
    onehot = (doc_ids[0][..., None] == doc_range).astype(jnp.float32)
    counts = lax.psum(jnp.sum(onehot, axis=1), "fsdp")
    inverse = 1.0 / (DOCS * counts)
    normed_all = normalize(hidden[0])
    master = weights[0].astype(jnp.float32)
    first = adam_m[0].astype(jnp.float32)
    second = adam_v[0].astype(jnp.float32)
    partial_losses = []
    for step_index in range(steps_total):
        normed = normed_all[step_index]
        columns = lax.all_to_all(normed, "fsdp", split_axis=1, concat_axis=0, tiled=True)
        current = master.astype(jnp.bfloat16)
        weight_row = jnp.dot(
            onehot[step_index], inverse[step_index], precision=lax.Precision.HIGHEST
        )
        empty = jnp.zeros((shard_rows, value_width), jnp.float32)

        def project(first_row, count, columns=columns, current=current):
            return jnp.dot(columns, current, preferred_element_type=jnp.float32)

        values = (
            lax.psum_scatter(
                project(jnp.int32(0), normed.shape[0] * lax.axis_size("fsdp")),
                "fsdp",
                scatter_dimension=0,
                tiled=True,
            )
            * scale
        )
        error = values - targets[0, step_index].astype(jnp.float32)
        partial_losses.append(jnp.sum(weight_row * 0.5 * jnp.mean(error * error, axis=-1)))
        error_grad = (weight_row[:, None] * error / value_width).astype(jnp.bfloat16)

        def accumulate(carry, piece, first_row, columns=columns):
            return lax.dot_general(
                columns, piece, (((0,), (0,)), ((), ())), preferred_element_type=jnp.float32
            )

        gradient = (
            accumulate(empty, lax.all_gather(error_grad, "fsdp", axis=0, tiled=True), jnp.int32(0))
            * scale
        )
        master, first, second = adam_update(master, first, second, gradient)
    losses = lax.psum(jnp.stack(partial_losses), "fsdp")
    merged = (
        MIXING * lax.dynamic_slice(master, (zero, start), (shard_rows, frag_width))
        + (1.0 - MIXING) * global_fragment
    )
    master = lax.dynamic_update_slice(master, merged, (zero, start))
    return (master[None], losses[None])


def solution(mesh):
    placed = (
        P("replica", None, "fsdp", None),
        P("replica", None, "fsdp", None),
        P("replica", None, "fsdp"),
        P("replica", "fsdp", None),
        P("replica", "fsdp", None),
        P("replica", "fsdp", None),
        P("fsdp", None),
        P("fsdp", None),
        P(),
    )
    return jax.shard_map(
        body,
        mesh=mesh,
        in_specs=placed,
        out_specs=(P("replica", "fsdp", None), P("replica", None)),
        check_vma=False,
    )
```

profile of v0, /device:TPU:0, one launch (start us, length us, event | category | flops | bytes accessed | tf_op | source)
XLA Modules:
  0.0 187.1 jit_solution(5239957921406506251)
XLA Ops:
  8.0 0.0 reduce-scatter.3.cloned.1.call-start
  8.0 2.1 %fusion.2 = f32[2,64]{1,0:T(2,128)S(1)} fusion(bf16[1,2,64,8192]{3,2,1,0:T(8,128)(2,1)} %param.9), kind=kLoop, calls=%fused_computation.6 | loop fusion | flops 3145600 | bytes 2097664 | tf_op jit(solution)/shard_map/reduce_sum | solution.py:22
  10.2 2.0 %fusion.3 = bf16[2,64,8192]{2,1,0:T(8,128)(2,1)S(1)} fusion(bf16[1,2,64,8192]{3,2,1,0:T(8,128)(2,1)} %param.9, f32[2,64]{1,0:T(2,128)S(1)} %add_rsqrt_fusion), kind=kLoop, calls=%fused_computation.7 | loop fusion | flops 3145728 | bytes 4194816 | tf_op jit(solution)/shard_map/convert_element_type | solution.py:23
  12.2 0.1 fusion.12
  12.4 0.8 all_to_all.28
  13.2 0.0 copy-start.4
  13.2 0.6 copy.15
  13.8 32.0 %all_to_all.38 = bf16[64,4,2048]{2,0,1:T(8,128)(2,1)S(1)} all-to-all(bf16[64,4,2048]{2,0,1:T(8,128)(2,1)S(1)} %copy.15), channel_id=1, replica_groups=mesh['replica'=8,'fsdp'=4] {'fsdp'}, dimensions={1} | all-to-all | bytes 2097152 | tf_op jit(solution)/shard_map/all_to_all | solution.py:65
  45.7 0.0 copy-done.4
  45.7 1.5 fusion.4
  47.2 0.0 copy-start.5
  47.2 0.0 copy-start.3
  47.2 0.0 reduce-scatter.3.cloned.1.call-update
  47.3 0.8 all_to_all.32
  48.1 1.6 copy.16
  49.6 3.5 %all-to-all-start.1 = ((bf16[64,4,2048]{2,0,1:T(8,128)(2,1)}), bf16[64,4,2048]{2,0,1:T(8,128)(2,1)S(1)}, u32[]{:S(2)}, u32[]{:S(2)}) async-start(bf16[64,4,2048]{2,0,1:T(8,128)(2,1)} %copy.16), calls=%async_computation.2 | async-start | bytes 2097152 | tf_op jit(solution)/shard_map/all_to_all | solution.py:65
  53.2 0.0 reduce-scatter.5.cloned.1.call-start
  53.2 0.0 copy-done.5
  53.2 0.1 convert_reduce_fusion
  53.3 30.4 %psum.21 = f32[2,8]{1,0:T(2,128)S(1)} all-reduce(f32[2,8]{1,0:T(2,128)S(1)} %convert_reduce_fusion), channel_id=1, replica_groups=mesh['replica'=8,'fsdp'=4] {'fsdp'}, use_global_device_ids=true, to_apply=%region_2.0 | all-reduce | flops 16 | bytes 128 | tf_op jit(solution)/shard_map/psum | solution.py:56
  83.8 0.1 convolution_bitcast_fusion.1
  83.9 0.0 reduce-scatter.3.cloned.1.call-done
  83.9 0.0 copy-done.3
  83.9 1.0 multiply_convert_fusion.1
  84.9 18.6 %all_gather.6 = bf16[256,512]{1,0:T(8,128)(2,1)S(1)} all-gather(bf16[64,512]{1,0:T(8,128)(2,1)S(1)} %multiply_convert_fusion.1), channel_id=1, replica_groups=mesh['replica'=8,'fsdp'=4] {'fsdp'}, dimensions={0}, use_global_device_ids=true | all-gather | bytes 327680 | tf_op jit(solution)/shard_map/all_gather | solution.py:94
  103.5 2.8 %fusion.13 = f32[2048,512]{1,0:T(8,128)} fusion(bf16[256,2048]{1,0:T(8,128)(2,1)S(1)} %bitcast.88, bf16[256,512]{1,0:T(8,128)(2,1)S(1)} %all_gather.6), kind=kOutput, calls=%fused_computation.41 | convolution fusion | flops 536870912 | bytes 5505024 | tf_op jit(solution)/shard_map/dot_general | solution.py:89
  106.2 0.0 all-to-all-done.1
  106.2 0.0 copy-start
  106.2 0.0 copy-start.2
  106.2 7.3 %fusion.6 = f32[256,512]{1,0:T(8,128)} fusion(bf16[256,2048]{1,0:T(8,128)(2,1)S(1)} %bitcast.90, f32[2048,512]{1,0:T(8,128)} %fusion.13, bf16[1,2048,512]{2,1,0:T(8,128)(2,1)} %param.13, bf16[1,2048,512]{2,1,0:T(8,128)(2,1)} %param.12, bf16[1,2048,512]{2,1,0:T(8,128)(2,1)} %param.14), kind=kOutput, calls=%fused_computation.13 | convolution fusion | flops 555745280 | bytes 12058624 | tf_op jit(solution)/shard_map/dot_general | solution.py:73
  113.5 0.0 reduce-scatter.5.cloned.1.call-update
  113.5 0.0 all-reduce.2.cloned.1.call-start
  114.2 0.0 copy-done
  114.2 2.2 %convert_subtract_fusion.2 = f32[2048,128]{1,0:T(8,128)} fusion(bf16[2048,128]{1,0:T(8,128)(2,1)S(1)} %copy-done, bf16[1,2048,512]{2,1,0:T(8,128)(2,1)} %param.12, s32[]{:T(128)S(6)} %select_n.2), kind=kLoop, calls=%fused_computation.16 | loop fusion | flops 786432 | bytes 2097156 | tf_op jit(solution)/shard_map/sub | solution.py:48
  116.4 0.0 all-reduce.2.cloned.1.call-update
  116.4 0.1 convolution_bitcast_fusion
  116.5 18.6 %reduce-scatter.5.cloned.1.call-done = f32[64,512]{1,0:T(8,128)} async-done(((f32[256,512]{1,0:T(8,128)}), f32[64,512]{1,0:T(8,128)}) %reduce-scatter.5.cloned.1.call-update) | async-done | bytes 131088 | tf_op jit(solution)/shard_map/reduce_scatter | solution.py:76
  135.2 0.0 copy-done.2
  135.2 1.1 multiply_reduce_fusion.1
  136.3 14.1 %all_gather.7 = bf16[256,512]{1,0:T(8,128)(2,1)S(1)} all-gather(bf16[64,512]{1,0:T(8,128)(2,1)S(1)} %get-tuple-element.6), channel_id=1, replica_groups=mesh['replica'=8,'fsdp'=4] {'fsdp'}, dimensions={0}, use_global_device_ids=true | all-gather | bytes 327680 | tf_op jit(solution)/shard_map/all_gather | solution.py:94
  150.4 0.7 multiply_reduce_fusion.2
  151.1 1.4 maximum_bitcast_fusion
  152.5 10.5 %multiply_subtract_fusion = f32[2048,512]{1,0:T(8,128)} fusion(f32[2048,512]{1,0:T(8,128)} %fusion.13, bf16[1,2048,512]{2,1,0:T(8,128)(2,1)} %param.13, bf16[1,2048,512]{2,1,0:T(8,128)(2,1)} %param.14, bf16[256,2048]{1,0:T(8,128)(2,1)S(1)} %bitcast.91, bf16[256,512]{1,0:T(8,128)(2,1)S(1)} %all_gather.7, bf16[1,2048,512]{2,1,0:T(8,128)(2,1)} %param.12), kind=kOutput, calls=%fused_computation.10 | convolution fusion | flops 569376768 | bytes 15990784 | tf_op jit(solution)/shard_map/dot_general | solution.py:89
  162.9 9.1 %psum.23 = f32[1,2]{1,0:T(1,128)} all-reduce(f32[1,2]{1,0:T(1,128)S(1)} %maximum_bitcast_fusion), channel_id=1, replica_groups=mesh['replica'=8,'fsdp'=4] {'fsdp'}, use_global_device_ids=true, to_apply=%region_10.0 | all-reduce | flops 2 | bytes 16 | tf_op jit(solution)/shard_map/psum | solution.py:98
  172.1 0.0 copy-start.1
  172.1 4.7 %copy.18 = f32[1,2048,512]{2,1,0:T(8,128)} copy(f32[1,2048,512]{2,1,0:T(8,128)} %bitcast.89) | data formatting | bytes 8388608
  176.8 0.0 copy-done.1
  176.8 2.9 %fusion.11 = f32[1,2048,512]{2,1,0:T(8,128)} fusion(f32[1,2048,512]{2,1,0:T(8,128)} %copy.18, s32[]{:T(128)S(6)} %select_n.2, bf16[2048,128]{1,0:T(8,128)(2,1)S(1)} %copy-done, bf16[2048,128]{1,0:T(8,128)(2,1)S(1)} %copy-done.1, f32[2048,128]{1,0:T(8,128)} %all-reduce.2.cloned.1.call-done, f32[2048,512]{1,0:T(8,128)} %multiply_subtract_fusion), kind=kLoop, calls=%fused_computation.22 | loop fusion | flops 2883584 | bytes 4194308 | tf_op jit(solution)/shard_map/dynamic_update_slice | solution.py:103
  (4 shorter events, 0.0 us)
Async XLA Ops:
  8.0 75.9 %reduce-scatter.3.cloned.1.call-start = ((), (), s32[]{:S(2)}) async-start(), calls=%async_computation.4 | async-start | bytes 655360 | tf_op jit(solution)/shard_map/reduce_scatter | solution.py:76
  13.2 32.6 %copy-start.4 = (bf16[1,2048,512]{2,1,0:T(8,128)(2,1)S(1)}, bf16[1,2048,512]{2,1,0:T(8,128)(2,1)}, u32[]{:S(2)}) copy-start(bf16[1,2048,512]{2,1,0:T(8,128)(2,1)} %param.12) | copy-start | bytes 6291460
  47.2 6.0 %copy-start.5 = (s32[1,2,64]{2,1,0:T(2,128)S(1)}, s32[1,2,64]{2,1,0:T(2,128)}, u32[]{:S(2)}) copy-start(s32[1,2,64]{2,1,0:T(2,128)} %param.11) | copy-start | bytes 1540
  47.2 36.6 %copy-start.3 = (bf16[1,2,64,512]{3,2,1,0:T(8,128)(2,1)S(1)}, bf16[1,2,64,512]{3,2,1,0:T(8,128)(2,1)}, u32[]{:S(2)}) copy-start(bf16[1,2,64,512]{3,2,1,0:T(8,128)(2,1)} %param.10) | copy-start | bytes 393220
  49.6 56.6 %all-to-all-start.1 = ((bf16[64,4,2048]{2,0,1:T(8,128)(2,1)}), bf16[64,4,2048]{2,0,1:T(8,128)(2,1)S(1)}, u32[]{:S(2)}, u32[]{:S(2)}) async-start(bf16[64,4,2048]{2,0,1:T(8,128)(2,1)} %copy.16), calls=%async_computation.2 | async-start | bytes 2097152 | tf_op jit(solution)/shard_map/all_to_all | solution.py:65
  53.2 82.0 %reduce-scatter.5.cloned.1.call-start = ((), (), s32[]{:S(2)}) async-start(), calls=%async_computation.5 | async-start | bytes 655360 | tf_op jit(solution)/shard_map/reduce_scatter | solution.py:76
  106.2 8.0 %copy-start = (bf16[2048,128]{1,0:T(8,128)(2,1)S(1)}, bf16[2048,128]{1,0:T(8,128)(2,1)}, u32[]{:S(2)}) copy-start(bf16[2048,128]{1,0:T(8,128)(2,1)} %param.15) | copy-start | bytes 1572868
  106.2 29.0 %copy-start.2 = (f32[64,512]{1,0:T(8,128)S(1)}, f32[64,512]{1,0:T(8,128)}, u32[]{:S(2)}) copy-start(f32[64,512]{1,0:T(8,128)} %reduce-scatter.3.cloned.1.call-done) | copy-start | bytes 393220
  113.5 63.3 %all-reduce.2.cloned.1.call-start = ((), (), s32[]{:S(2)}) async-start(), calls=%async_computation.6 | async-start | bytes 2097152 | tf_op jit(solution)/shard_map/psum | solution.py:50
  172.1 4.7 %copy-start.1 = (bf16[2048,128]{1,0:T(8,128)(2,1)S(1)}, bf16[2048,128]{1,0:T(8,128)(2,1)}, u32[]{:S(2)}) copy-start(bf16[2048,128]{1,0:T(8,128)(2,1)} %param.16) | copy-start | bytes 1572868
Sparse Core Ops, SparseCore 0:
  47.4 26.2 reduce-scatter.2
  113.6 21.4 reduce-scatter.4
Sparse Core Ops, SparseCore 1:
  117.1 55.9 all-reduce.1
where the time goes:
time: 188 us; the launch traced here: 187 us
  blocking collectives  104 us (55%)
  matrix products  22.2 us (12%)
  waiting for transfers between devices  18.7 us (10%)
  between operations  16.2 us (9%)
  other arithmetic  13.5 us (7%)
  local copies, waits for them, and re-layouts  8.62 us (5%)
  starting transfers between devices  3.65 us (2%)
    all_gather x2, blocking collectives, body(): lax.all_gather(error_grad, 'fsdp', axis=0, tiled=True)  32.7 us
    all_to_all x1, blocking collectives, body(): lax.all_to_all(normed, 'fsdp', split_axis=1, concat_axis=0, tiled=True)  32 us
    psum x1, blocking collectives, body(): counts = lax.psum(jnp.sum(onehot, axis=1), 'fsdp')  30.4 us
    reduce_scatter x2, waiting for transfers between devices, body(): lax.psum_scatter(project(jnp.int32(0), normed.shape[0] * lax.axis_size('f...  18.6 us
    dot_general x2, matrix products, accumulate(): lax.dot_general(columns, piece, (((0,), (0,)), ((), ())), preferred_eleme...  13.2 us
    psum x1, blocking collectives, body(): losses = lax.psum(jnp.stack(partial_losses), 'fsdp')  9.15 us
    dot_general x2, matrix products, project(): return jnp.dot(columns, current, preferred_element_type=jnp.float32)  8.78 us
    unnamed x13, local copies, waits for them, and re-layouts  4.72 us
  transfers between devices with their start and end apart: 4, of which 1 were waited for; matrix products, arithmetic and copies ran while one was open for 14% of the time, Pallas kernels for 0%

commit v1 on v0

v1 whole, which is shorter than its diff:
```python
import functools

import jax
import jax.numpy as jnp
from jax import lax
from jax.experimental import pallas as pl
from jax.experimental.pallas import tpu as pltpu
from jax.sharding import PartitionSpec as P

DOCS = 8
NORM_EPS = 1e-05
ADAM_EPS = 1e-08
INNER_RATE = 0.1
DECAY_RATE = 0.1
BETA_FIRST = 0.9
BETA_SECOND = 0.95
OUTER_RATE = 0.7
NESTEROV = 0.9
MIXING = 0.5
LANES = 128
MESH = pl.DeviceIdType.MESH
F32 = jnp.float32
BF16 = jnp.bfloat16


def adam_update(master, first, second, gradient):
    first = BETA_FIRST * first + (1.0 - BETA_FIRST) * gradient
    second = BETA_SECOND * second + (1.0 - BETA_SECOND) * gradient * gradient
    master = master - INNER_RATE * (first / (jnp.sqrt(second) + ADAM_EPS) + DECAY_RATE * master)
    return (master, first, second)


def partners(me, n):
    if n == 4:
        return [lax.rem(me + 2, 4), 3 - me, me + 1 - 2 * lax.rem(me, 2)]
    return [lax.rem(me + k, n) for k in range(1, n)]


def window_kernel(
    n, replicas, dims,
    hidden, targets, doc_ids, weights, adam_m, adam_v, anchor, momentum, fragment,
    master_out, first_out, second_out, turned_out, grads_out, frag_out, loss_out,
    cols, hid, w_ref, m_ref, v_ref, current, master, first, second, turned,
    partial, part_send, part_recv, grads, counts, losses,
    frag_cols, frag_recv, frag_all, anchor_ref, moment_ref, row_scale, token_weight,
    local_sem, out_sem, a2a_send, a2a_recv, count_send, count_recv,
    frag_send, frag_got, all_send, all_got, part_send_sem, part_recv_sem,
    grad_send, grad_recv, loss_send, loss_recv,
):
    steps, tokens, rows, width, model, fw = dims
    own = rows // replicas
    scale = model ** (-0.5)
    rep = lax.axis_index("replica")
    me = lax.axis_index("fsdp")
    others = partners(me, n)
    peers = [lax.rem(rep + k, replicas) for k in range(1, replicas)]

    def block(index, size):
        return pl.ds(pl.multiple_of(index * size, size), size)

    my_tokens = block(me, tokens)
    my_frag = block(rep, own)

    local = [
        pltpu.make_async_copy(weights.at[0], w_ref, local_sem.at[0]),
        pltpu.make_async_copy(hidden.at[0], hid, local_sem.at[1]),
        pltpu.make_async_copy(anchor.at[my_frag, :], anchor_ref, local_sem.at[2]),
        pltpu.make_async_copy(momentum.at[my_frag, :], moment_ref, local_sem.at[3]),
        pltpu.make_async_copy(adam_m.at[0], m_ref, local_sem.at[4]),
        pltpu.make_async_copy(adam_v.at[0], v_ref, local_sem.at[5]),
    ]
    for s in range(steps):
        local.append(pltpu.make_async_copy(
            hidden.at[0, s, :, block(me, rows)], cols.at[s, my_tokens, :], local_sem.at[6 + s]))
    for copy in local:
        copy.start()

    barrier = pltpu.get_barrier_semaphore()
    for j in others:
        pl.semaphore_signal(barrier, inc=1, device_id=(rep, j), device_id_type=MESH)
    for i in peers:
        pl.semaphore_signal(barrier, inc=1, device_id=(i, me), device_id_type=MESH)
    pl.semaphore_wait(barrier, n + replicas - 2)

    def a2a(s, j):
        return pltpu.make_async_remote_copy(
            src_ref=hidden.at[0, s, :, block(j, rows)], dst_ref=cols.at[s, my_tokens, :],
            send_sem=a2a_send.at[s, j], recv_sem=a2a_recv.at[s, me],
            device_id=(rep, j), device_id_type=MESH)

    def a2a_arrived(s, j):
        pltpu.make_async_remote_copy(
            src_ref=hidden.at[0, s, :, block(j, rows)], dst_ref=cols.at[s, block(j, tokens), :],
            send_sem=a2a_send.at[s, j], recv_sem=a2a_recv.at[s, j],
            device_id=(rep, j), device_id_type=MESH).wait_recv()

    for j in others:
        a2a(0, j).start()

    lane = lax.broadcasted_iota(jnp.int32, (tokens, LANES), 1).astype(F32)
    eye = (lax.broadcasted_iota(jnp.int32, (tokens, tokens), 0)
           == lax.broadcasted_iota(jnp.int32, (tokens, tokens), 1))
    onehots = []
    row8 = lax.broadcasted_iota(jnp.int32, (8, LANES), 0)
    tally = jnp.zeros((8, LANES), F32)
    for s in range(steps):
        ids = jnp.broadcast_to(doc_ids[0, s:s + 1, :].astype(F32), (tokens, tokens))
        ids = jnp.sum(jnp.where(eye, ids, 0.0), axis=1, keepdims=True)
        onehot = (ids == lane).astype(F32)
        onehots.append(onehot)
        tally = tally + jnp.where(row8 == s, jnp.sum(onehot, axis=0, keepdims=True), 0.0)
    counts[me] = tally

    def to_all(buf, send, recv, j):
        return pltpu.make_async_remote_copy(
            src_ref=buf.at[me], dst_ref=buf.at[me], send_sem=send.at[j], recv_sem=recv.at[me],
            device_id=(rep, j), device_id_type=MESH)

    def from_all(buf, send, recv, j):
        pltpu.make_async_remote_copy(
            src_ref=buf.at[j], dst_ref=buf.at[j], send_sem=send.at[j], recv_sem=recv.at[j],
            device_id=(rep, j), device_id_type=MESH).wait_recv()

    for j in others:
        to_all(counts, count_send, count_recv, j).start()

    local[0].wait()
    picked = fragment[0]
    for k in range(width // fw):
        piece = w_ref[:, k * fw:(k + 1) * fw]
        if k == 0:
            frag_cols[...] = piece
        else:
            frag_cols[...] = jnp.where(picked == k, piece, frag_cols[...])

    def frag_copy(i):
        return pltpu.make_async_remote_copy(
            src_ref=frag_cols.at[block(i, own), :], dst_ref=frag_recv.at[rep],
            send_sem=frag_send.at[i], recv_sem=frag_got.at[rep],
            device_id=(i, me), device_id_type=MESH)

    for i in peers:
        frag_copy(i).start()
    frag_recv[rep] = frag_cols[my_frag, :]

    local[1].wait()
    wide = 4 * LANES
    for s in range(steps):
        def add_squares(c, acc, s=s):
            x = hid[s, :, block(c, wide)].astype(F32)
            return acc + x * x
        acc = lax.fori_loop(0, model // wide, add_squares, jnp.zeros((tokens, wide), F32))
        power = jnp.sum(acc, axis=1, keepdims=True) / model
        row_scale[s] = jnp.broadcast_to(lax.rsqrt(power + NORM_EPS), (tokens, LANES))

    for j in others:
        from_all(counts, count_send, count_recv, j)
    total = counts[0]
    for j in range(1, n):
        total = total + counts[j]
    inverse = jnp.where(total > 0.0, 1.0 / (DOCS * jnp.maximum(total, 1.0)), 0.0)
    for s in range(steps):
        weight = jnp.sum(onehots[s] * inverse[s:s + 1, :], axis=1, keepdims=True)
        token_weight[s] = jnp.broadcast_to(weight, (tokens, LANES))

    for i in peers:
        pltpu.make_async_remote_copy(
            src_ref=frag_recv.at[i], dst_ref=frag_recv.at[i], send_sem=frag_send.at[i],
            recv_sem=frag_got.at[i], device_id=(i, me), device_id_type=MESH).wait_recv()
    local[2].wait()
    local[3].wait()
    base = anchor_ref[...].astype(F32)
    delta = base - frag_recv[0].astype(F32)
    for i in range(1, replicas):
        delta = delta + (base - frag_recv[i].astype(F32))
    mean_delta = delta / replicas
    new_moment = NESTEROV * moment_ref[...].astype(F32) + mean_delta
    frag_all[my_frag, :] = base - OUTER_RATE * (mean_delta + NESTEROV * new_moment)

    def all_copy(i):
        return pltpu.make_async_remote_copy(
            src_ref=frag_all.at[my_frag, :], dst_ref=frag_all.at[my_frag, :],
            send_sem=all_send.at[i], recv_sem=all_got.at[rep],
            device_id=(i, me), device_id_type=MESH)

    for i in peers:
        all_copy(i).start()

    for j in others:
        a2a(0, j).wait_send()
        a2a(1, j).start()

    def part_copy(s, j):
        return pltpu.make_async_remote_copy(
            src_ref=part_send.at[s, block(j, tokens), :], dst_ref=part_recv.at[s, me],
            send_sem=part_send_sem.at[s, j], recv_sem=part_recv_sem.at[s, me],
            device_id=(rep, j), device_id_type=MESH)

    def grad_copy(s, j):
        return pltpu.make_async_remote_copy(
            src_ref=grads.at[s, my_tokens, :], dst_ref=grads.at[s, my_tokens, :],
            send_sem=grad_send.at[s, j], recv_sem=grad_recv.at[s, me],
            device_id=(rep, j), device_id_type=MESH)

    tile = 256

    def project_and_share(s, held):
        for j in others:
            a2a_arrived(s, j)
        local[6 + s].wait()

        @pl.loop(0, width // tile)
        def _(c):
            at = block(c, tile)
            out = jnp.dot(cols[s], held[:, at], preferred_element_type=F32)
            partial[:, at] = out
            part_send[s, :, at] = out.astype(BF16)

        for j in others:
            part_copy(s, j).start()

        @pl.loop(0, rows // tile)
        def _(c):
            at = block(c, tile)
            turned[s, at, :] = cols[s, :, at].T

        values = partial[my_tokens, :]
        for j in others:
            pltpu.make_async_remote_copy(
                src_ref=part_recv.at[s, j], dst_ref=part_recv.at[s, j],
                send_sem=part_send_sem.at[s, j], recv_sem=part_recv_sem.at[s, j],
                device_id=(rep, j), device_id_type=MESH).wait_recv()
            values = values + part_recv[s, j].astype(F32)
        gain = row_scale[s][:, :1]
        weight = token_weight[s][:, :1]
        error = values * (gain * scale) - targets[0, s].astype(F32)
        grads[s, my_tokens, :] = ((weight * gain / width) * error).astype(BF16)
        for j in others:
            grad_copy(s, j).start()
        loss = jnp.sum(weight * 0.5 * jnp.mean(error * error, axis=-1, keepdims=True))
        loss = jnp.where(row8 == s, loss, 0.0)
        if s == 0:
            losses[me] = loss
        else:
            losses[me] = losses[me] + loss
        if s == steps - 1:
            for j in others:
                to_all(losses, loss_send, loss_recv, j).start()
        for j in others:
            pltpu.make_async_remote_copy(
                src_ref=grads.at[s, block(j, tokens), :], dst_ref=grads.at[s, block(j, tokens), :],
                send_sem=grad_send.at[s, j], recv_sem=grad_recv.at[s, j],
                device_id=(rep, j), device_id_type=MESH).wait_recv()

    project_and_share(0, w_ref)
    local[4].wait()
    local[5].wait()
    rt = 128

    @pl.loop(0, rows // rt)
    def _(c):
        at = block(c, rt)
        gradient = jnp.dot(turned[0, at, :], grads[0], preferred_element_type=F32) * scale
        new_master, new_first, new_second = adam_update(
            w_ref[at, :].astype(F32), m_ref[at, :].astype(F32), v_ref[at, :].astype(F32), gradient)
        master[at, :] = new_master
        first[at, :] = new_first
        second[at, :] = new_second
        current[at, :] = new_master.astype(BF16)

    outs = [
        pltpu.make_async_copy(master, master_out, out_sem.at[0]),
        pltpu.make_async_copy(first, first_out, out_sem.at[1]),
        pltpu.make_async_copy(second, second_out, out_sem.at[2]),
    ]
    for copy in outs:
        copy.start()
    for i in peers:
        at = block(i, own)
        pltpu.make_async_remote_copy(
            src_ref=frag_all.at[at, :], dst_ref=frag_all.at[at, :], send_sem=all_send.at[i],
            recv_sem=all_got.at[i], device_id=(i, me), device_id_type=MESH).wait_recv()
    outs.append(pltpu.make_async_copy(frag_all, frag_out, out_sem.at[3]))
    outs[-1].start()

    project_and_share(1, current)
    outs.append(pltpu.make_async_copy(turned.at[1], turned_out, out_sem.at[4]))
    outs.append(pltpu.make_async_copy(grads.at[1], grads_out, out_sem.at[5]))
    outs[-2].start()
    outs[-1].start()
    for j in others:
        from_all(losses, loss_send, loss_recv, j)
    loss = losses[0]
    for j in range(1, n):
        loss = loss + losses[j]
    loss_out[...] = loss

    for j in others:
        a2a(1, j).wait_send()
        to_all(counts, count_send, count_recv, j).wait_send()
        to_all(losses, loss_send, loss_recv, j).wait_send()
        for s in range(steps):
            part_copy(s, j).wait_send()
            grad_copy(s, j).wait_send()
    for i in peers:
        frag_copy(i).wait_send()
        all_copy(i).wait_send()
    for copy in outs:
        copy.wait()


def finish_kernel(scale, fw, fragment, master, first, second, turned, grads, frag, loss,
                  out, loss_out):
    gradient = jnp.dot(turned[...], grads[...], preferred_element_type=F32) * scale
    new_master, _, _ = adam_update(master[...], first[...], second[...], gradient)
    picked = fragment[0]
    mixed = (1.0 - MIXING) * frag[...]
    for k in range(out.shape[2] // fw):
        piece = new_master[:, k * fw:(k + 1) * fw]
        out[0, :, k * fw:(k + 1) * fw] = jnp.where(picked == k, MIXING * piece + mixed, piece)
    steps = loss_out.shape[1]
    across = lax.broadcasted_iota(jnp.int32, (1, steps), 1)
    line = jnp.zeros((1, steps), F32)
    for s in range(steps):
        line = jnp.where(across == s, loss[s:s + 1, :steps], line)
    loss_out[...] = line


def body(n, replicas, hidden, targets, doc_ids, weights, adam_m, adam_v, anchor, momentum, fragment):
    steps, tokens, model = hidden.shape[1:]
    rows, width = weights.shape[1:]
    fw = anchor.shape[1]
    own = rows // replicas
    everyone = n * tokens
    dims = (steps, tokens, rows, width, model, fw)
    any_spec = pl.BlockSpec(memory_space=pl.ANY)
    vmem = pl.BlockSpec(memory_space=pltpu.VMEM)
    smem = pl.BlockSpec(memory_space=pltpu.SMEM)
    dma = pltpu.SemaphoreType.DMA
    shape = jax.ShapeDtypeStruct
    master, first, second, turned, grads, frag, loss = pl.pallas_call(
        functools.partial(window_kernel, n, replicas, dims),
        out_shape=[
            shape((rows, width), F32), shape((rows, width), F32), shape((rows, width), F32),
            shape((rows, everyone), BF16), shape((everyone, width), BF16),
            shape((rows, fw), F32), shape((8, LANES), F32),
        ],
        in_specs=[any_spec, vmem, vmem, any_spec, any_spec, any_spec, any_spec, any_spec, smem],
        out_specs=[any_spec] * 6 + [vmem],
        scratch_shapes=[
            pltpu.VMEM((steps, everyone, rows), BF16),
            pltpu.VMEM((steps, tokens, model), BF16),
            pltpu.VMEM((rows, width), BF16),
            pltpu.VMEM((rows, width), BF16),
            pltpu.VMEM((rows, width), BF16),
            pltpu.VMEM((rows, width), BF16),
            pltpu.VMEM((rows, width), F32),
            pltpu.VMEM((rows, width), F32),
            pltpu.VMEM((rows, width), F32),
            pltpu.VMEM((steps, rows, everyone), BF16),
            pltpu.VMEM((everyone, width), F32),
            pltpu.VMEM((steps, everyone, width), BF16),
            pltpu.VMEM((steps, n, tokens, width), BF16),
            pltpu.VMEM((steps, everyone, width), BF16),
            pltpu.VMEM((n, 8, LANES), F32),
            pltpu.VMEM((n, 8, LANES), F32),
            pltpu.VMEM((rows, fw), BF16),
            pltpu.VMEM((replicas, own, fw), BF16),
            pltpu.VMEM((rows, fw), F32),
            pltpu.VMEM((own, fw), BF16),
            pltpu.VMEM((own, fw), BF16),
            pltpu.VMEM((steps, tokens, LANES), F32),
            pltpu.VMEM((steps, tokens, LANES), F32),
            dma((6 + steps,)), dma((6,)),
            dma((steps, n)), dma((steps, n)), dma((n,)), dma((n,)),
            dma((replicas,)), dma((replicas,)), dma((replicas,)), dma((replicas,)),
            dma((steps, n)), dma((steps, n)),
            dma((steps, n)), dma((steps, n)), dma((n,)), dma((n,)),
        ],
        compiler_params=pltpu.CompilerParams(
            collective_id=0, has_side_effects=True, vmem_limit_bytes=52 * 1024 * 1024),
        name="window",
    )(hidden, targets, doc_ids, weights, adam_m, adam_v, anchor, momentum, fragment)

    rt = min(256, rows)
    whole = lambda shape: pl.BlockSpec(shape, lambda i: (0, 0))
    piece = lambda cols: pl.BlockSpec((rt, cols), lambda i: (i, 0))
    return pl.pallas_call(
        functools.partial(finish_kernel, model ** (-0.5), fw),
        grid=(rows // rt,),
        out_shape=[shape((1, rows, width), F32), shape((1, steps), F32)],
        in_specs=[smem, piece(width), piece(width), piece(width), piece(everyone),
                  whole((everyone, width)), piece(fw), whole((8, LANES))],
        out_specs=[pl.BlockSpec((1, rt, width), lambda i: (0, i, 0)), whole((1, steps))],
        compiler_params=pltpu.CompilerParams(vmem_limit_bytes=32 * 1024 * 1024),
        name="finish",
    )(fragment, master, first, second, turned, grads, frag, loss)


def solution(mesh):
    placed = (
        P("replica", None, "fsdp", None),
        P("replica", None, "fsdp", None),
        P("replica", None, "fsdp"),
        P("replica", "fsdp", None),
        P("replica", "fsdp", None),
        P("replica", "fsdp", None),
        P("fsdp", None),
        P("fsdp", None),
        P(),
    )
    return jax.shard_map(
        functools.partial(body, mesh.shape["fsdp"], mesh.shape["replica"]),
        mesh=mesh,
        in_specs=placed,
        out_specs=(P("replica", "fsdp", None), P("replica", None)),
        check_vma=False,
    )
```

time: 188 us -> 111 us (0.59)
  blocking collectives: 104 us -> 0 us
  Pallas kernels: 0 us -> 96.3 us
  matrix products: 22.2 us -> 0 us
  waiting for transfers between devices: 18.7 us -> 0 us
  between operations: 16.2 us -> 1.31 us
  other arithmetic: 13.5 us -> 0 us
  local copies, waits for them, and re-layouts: 8.62 us -> 12.7 us
  starting transfers between devices: 3.65 us -> 0 us
    pallas_call x0 -> x2, Pallas kernels: none -> 96.3 us  [the longest x1 90.1 us: body(): pl.pallas_call(functools.partial(window_kernel, n, replicas, dims), out_s...]
    psum x2 -> x0, blocking collectives: 39.6 us -> none  [the longest x1 30.4 us: body(): counts = lax.psum(jnp.sum(onehot, axis=1), 'fsdp')]
    all_gather x2 -> x0, blocking collectives: 32.7 us -> none  [body(): lax.all_gather(error_grad, 'fsdp', axis=0, tiled=True)]
    all_to_all x1 -> x0, blocking collectives: 32 us -> none  [body(): lax.all_to_all(normed, 'fsdp', split_axis=1, concat_axis=0, tiled=True)]
    dot_general x6 -> x0, matrix products: 22.2 us -> none  [the longest x2 13.2 us: accumulate(): lax.dot_general(columns, piece, (((0,), (0,)), ((), ())), preferred_eleme...]
    reduce_scatter x2 -> x0, waiting for transfers between devices: 18.6 us -> none  [body(): lax.psum_scatter(project(jnp.int32(0), normed.shape[0] * lax.axis_size('f...]
    unnamed x13 -> x18, local copies, waits for them, and re-layouts: 4.72 us -> 12.7 us
    reduce_sum x4 -> x0, other arithmetic: 3.97 us -> none  [the longest x1 2.11 us: normalize(): power = jnp.mean(wide * wide, axis=-1, keepdims=True)]
  transfers between devices with their start and end apart: 4 -> 0, of which waited for: 1 -> 0; matrix products, arithmetic and copies ran while one was open for 14% -> 0% of each run, Pallas kernels for 0% -> 0%
where the time goes in v1:
time: 111 us; the launch traced here: 110 us
  Pallas kernels  96.3 us (87%)
  local copies, waits for them, and re-layouts  12.7 us (11%)
  between operations  1.31 us (1%)
    pallas_call x1, Pallas kernels, body(): pl.pallas_call(functools.partial(window_kernel, n, replicas, dims), out_s...  90.1 us
    unnamed x18, local copies, waits for them, and re-layouts  12.7 us
    pallas_call x1, Pallas kernels, body(): pl.pallas_call(functools.partial(finish_kernel, model ** (-0.5), fw), gri...  6.21 us

profile of v1, /device:TPU:0, one launch (start us, length us, event | category | flops | bytes accessed | tf_op | source)
XLA Modules:
  0.0 110.3 jit_solution(9974367350332865124)
XLA Ops:
  1.3 0.0 copy-start.5
  1.3 1.0 copy-done.5
  2.3 0.0 copy-start.6
  2.3 1.0 copy-done.6
  3.4 0.0 copy-start.7
  3.4 0.9 copy-done.7
  4.3 0.0 copy-start.8
  4.3 0.7 copy-done.8
  4.9 90.1 %window.1 = (f32[2048,512]{1,0:T(8,128)}, f32[2048,512]{1,0:T(8,128)}, f32[2048,512]{1,0:T(8,128)}, bf16[2048,256]{1,0:T(8,128)(2,1)}, bf16[256,512]{1,0:T(8,128...) custom-call(bf16[1,2,64,8192]{3,2,1,0:T(8,128)(2,1)} %hidden.1, bf16[1,2,64,512]{3,2,1,0:T(8,128)(2,1)S(1)} %copy-done.7, ...), custom_call_target="tpu_custom_call" | custom-call | tf_op jit(solution)/shard_map/window/pallas_call | solution.py:341
  95.1 0.0 copy-start
  95.1 2.2 %copy-done = f32[2048,512]{1,0:T(8,128)S(1)} copy-done((f32[2048,512]{1,0:T(8,128)S(1)}, f32[2048,512]{1,0:T(8,128)}, u32[]{:S(2)}) %copy-start) | copy-done | bytes 4194328
  97.3 0.0 copy-start.1
  97.3 2.2 %copy-done.1 = f32[2048,512]{1,0:T(8,128)S(1)} copy-done((f32[2048,512]{1,0:T(8,128)S(1)}, f32[2048,512]{1,0:T(8,128)}, u32[]{:S(2)}) %copy-start.1) | copy-done | bytes 4194328
  99.4 0.0 copy-start.2
  99.4 2.2 %copy-done.2 = f32[2048,512]{1,0:T(8,128)S(1)} copy-done((f32[2048,512]{1,0:T(8,128)S(1)}, f32[2048,512]{1,0:T(8,128)}, u32[]{:S(2)}) %copy-start.2) | copy-done | bytes 4194328
  101.6 0.0 copy-start.3
  101.6 1.2 %copy-done.3 = bf16[2048,256]{1,0:T(8,128)(2,1)S(1)} copy-done((bf16[2048,256]{1,0:T(8,128)(2,1)S(1)}, bf16[2048,256]{1,0:T(8,128)(2,1)}, u32[]{:S(2)}) %copy-start.3) | copy-done | bytes 1048600
  102.9 0.0 copy-start.4
  102.9 1.2 %copy-done.4 = f32[2048,128]{1,0:T(8,128)S(1)} copy-done((f32[2048,128]{1,0:T(8,128)S(1)}, f32[2048,128]{1,0:T(8,128)}, u32[]{:S(2)}) %copy-start.4) | copy-done | bytes 1048600
  104.1 6.2 %finish.1 = (f32[1,2048,512]{2,1,0:T(8,128)}, f32[1,2]{1,0:T(1,128)}) custom-call(s32[1]{0:T(128)S(6)} %copy.11.fragment, f32[2048,512]{1,0:T(8,128)S(1)} %copy-done, f32[2048,512]{1,0:T(8,128)S(1)} %copy-done.1, f32[2048,512]{1,0:T(8,128)S(1)} %copy-done.2, bf16[2048,256]{1,0:T(8,128)(2,1)S(1)} %copy-done.3, bf16[256,512]{1,0:T(8,128)(2,1)S(1)} %get-tuple-element.13.grads, ...), custom_call_target="tpu_custom_call" | custom-call | tf_op jit(solution)/shard_map/finish/pallas_call | solution.py:388
Async XLA Ops:
  1.3 1.0 copy-start.5
  2.3 1.0 copy-start.6
  3.4 0.9 copy-start.7
  4.3 0.7 copy-start.8
  95.1 2.2 %copy-start = (f32[2048,512]{1,0:T(8,128)S(1)}, f32[2048,512]{1,0:T(8,128)}, u32[]{:S(2)}) copy-start(f32[2048,512]{1,0:T(8,128)} %get-tuple-element.9.master) | copy-start | bytes 12582916
  97.3 2.2 %copy-start.1 = (f32[2048,512]{1,0:T(8,128)S(1)}, f32[2048,512]{1,0:T(8,128)}, u32[]{:S(2)}) copy-start(f32[2048,512]{1,0:T(8,128)} %get-tuple-element.10.first) | copy-start | bytes 12582916
  99.4 2.2 %copy-start.2 = (f32[2048,512]{1,0:T(8,128)S(1)}, f32[2048,512]{1,0:T(8,128)}, u32[]{:S(2)}) copy-start(f32[2048,512]{1,0:T(8,128)} %get-tuple-element.11.second) | copy-start | bytes 12582916
  101.6 1.2 %copy-start.3 = (bf16[2048,256]{1,0:T(8,128)(2,1)S(1)}, bf16[2048,256]{1,0:T(8,128)(2,1)}, u32[]{:S(2)}) copy-start(bf16[2048,256]{1,0:T(8,128)(2,1)} %get-tuple-element.12.turned) | copy-start | bytes 3145732
  102.9 1.2 %copy-start.4 = (f32[2048,128]{1,0:T(8,128)S(1)}, f32[2048,128]{1,0:T(8,128)}, u32[]{:S(2)}) copy-start(f32[2048,128]{1,0:T(8,128)} %get-tuple-element.14.frag) | copy-start | bytes 3145732

commit v2 on v1

--- a/solution.py
+++ b/solution.py
@@ -38,9 +38,9 @@
 
 def window_kernel(
     n, replicas, dims,
-    hidden, targets, doc_ids, weights, adam_m, adam_v, anchor, momentum, fragment,
-    master_out, first_out, second_out, turned_out, grads_out, frag_out, loss_out,
-    cols, hid, w_ref, m_ref, v_ref, current, master, first, second, turned,
+    hidden, targets_in, ids_in, weights, adam_m, adam_v, anchor, momentum, fragment,
+    master_out, first_out, second_out, turned_out, grads_out, loss_out,
+    cols, hid, targets, doc_ids, w_ref, m_ref, v_ref, current, master, first, second, turned,
     partial, part_send, part_recv, grads, counts, losses,
     frag_cols, frag_recv, frag_all, anchor_ref, moment_ref, row_scale, token_weight,
     local_sem, out_sem, a2a_send, a2a_recv, count_send, count_recv,
@@ -72,6 +72,8 @@
     for s in range(steps):
         local.append(pltpu.make_async_copy(
             hidden.at[0, s, :, block(me, rows)], cols.at[s, my_tokens, :], local_sem.at[6 + s]))
+    local.append(pltpu.make_async_copy(targets_in, targets, local_sem.at[6 + steps]))
+    local.append(pltpu.make_async_copy(ids_in, doc_ids, local_sem.at[7 + steps]))
     for copy in local:
         copy.start()
 
@@ -97,6 +99,7 @@
     for j in others:
         a2a(0, j).start()
 
+    local[7 + steps].wait()
     lane = lax.broadcasted_iota(jnp.int32, (tokens, LANES), 1).astype(F32)
     eye = (lax.broadcasted_iota(jnp.int32, (tokens, tokens), 0)
            == lax.broadcasted_iota(jnp.int32, (tokens, tokens), 1))
@@ -185,6 +188,8 @@
 
     for i in peers:
         all_copy(i).start()
+
+    local[6 + steps].wait()
 
     for j in others:
         a2a(0, j).wait_send()
@@ -257,16 +262,26 @@
     local[5].wait()
     rt = 128
 
+    for i in peers:
+        at = block(i, own)
+        pltpu.make_async_remote_copy(
+            src_ref=frag_all.at[at, :], dst_ref=frag_all.at[at, :], send_sem=all_send.at[i],
+            recv_sem=all_got.at[i], device_id=(i, me), device_id_type=MESH).wait_recv()
+
     @pl.loop(0, rows // rt)
     def _(c):
         at = block(c, rt)
         gradient = jnp.dot(turned[0, at, :], grads[0], preferred_element_type=F32) * scale
         new_master, new_first, new_second = adam_update(
             w_ref[at, :].astype(F32), m_ref[at, :].astype(F32), v_ref[at, :].astype(F32), gradient)
-        master[at, :] = new_master
-        first[at, :] = new_first
-        second[at, :] = new_second
         current[at, :] = new_master.astype(BF16)
+        first[at, :] = (INNER_RATE * BETA_FIRST) * new_first
+        second[at, :] = BETA_SECOND * new_second
+        kept = (1.0 - INNER_RATE * DECAY_RATE) * new_master
+        mixed = (1.0 - MIXING) * frag_all[at, :]
+        for k in range(width // fw):
+            piece = kept[:, k * fw:(k + 1) * fw]
+            master[at, k * fw:(k + 1) * fw] = jnp.where(picked == k, MIXING * piece + mixed, piece)
 
     outs = [
         pltpu.make_async_copy(master, master_out, out_sem.at[0]),
@@ -275,17 +290,10 @@
     ]
     for copy in outs:
         copy.start()
-    for i in peers:
-        at = block(i, own)
-        pltpu.make_async_remote_copy(
-            src_ref=frag_all.at[at, :], dst_ref=frag_all.at[at, :], send_sem=all_send.at[i],
-            recv_sem=all_got.at[i], device_id=(i, me), device_id_type=MESH).wait_recv()
-    outs.append(pltpu.make_async_copy(frag_all, frag_out, out_sem.at[3]))
-    outs[-1].start()
 
     project_and_share(1, current)
-    outs.append(pltpu.make_async_copy(turned.at[1], turned_out, out_sem.at[4]))
-    outs.append(pltpu.make_async_copy(grads.at[1], grads_out, out_sem.at[5]))
+    outs.append(pltpu.make_async_copy(turned.at[1], turned_out, out_sem.at[3]))
+    outs.append(pltpu.make_async_copy(grads.at[1], grads_out, out_sem.at[4]))
     outs[-2].start()
     outs[-1].start()
     for j in others:
@@ -309,15 +317,15 @@
         copy.wait()
 
 
-def finish_kernel(scale, fw, fragment, master, first, second, turned, grads, frag, loss,
-                  out, loss_out):
-    gradient = jnp.dot(turned[...], grads[...], preferred_element_type=F32) * scale
-    new_master, _, _ = adam_update(master[...], first[...], second[...], gradient)
-    picked = fragment[0]
-    mixed = (1.0 - MIXING) * frag[...]
-    for k in range(out.shape[2] // fw):
-        piece = new_master[:, k * fw:(k + 1) * fw]
-        out[0, :, k * fw:(k + 1) * fw] = jnp.where(picked == k, MIXING * piece + mixed, piece)
+def finish_kernel(scale, fw, fragment, kept, first, second, turned, grads, loss, out, loss_out):
+    raw = jnp.dot(turned[...], grads[...], preferred_element_type=F32)
+    moved = first[...] + (INNER_RATE * (1.0 - BETA_FIRST) * scale) * raw
+    power = second[...] + ((1.0 - BETA_SECOND) * scale * scale) * (raw * raw)
+    step = moved / (power * lax.rsqrt(power) + ADAM_EPS)
+    width = out.shape[2]
+    column = lax.broadcasted_iota(jnp.int32, (1, width), 1) // fw
+    share = jnp.where(column == fragment[0], MIXING, 1.0)
+    out[0] = kept[...] - share * step
     steps = loss_out.shape[1]
     across = lax.broadcasted_iota(jnp.int32, (1, steps), 1)
     line = jnp.zeros((1, steps), F32)
@@ -333,23 +341,25 @@
     own = rows // replicas
     everyone = n * tokens
     dims = (steps, tokens, rows, width, model, fw)
-    any_spec = pl.BlockSpec(memory_space=pl.ANY)
+    any_spec = pl.BlockSpec(memory_space=pltpu.HBM)
     vmem = pl.BlockSpec(memory_space=pltpu.VMEM)
     smem = pl.BlockSpec(memory_space=pltpu.SMEM)
     dma = pltpu.SemaphoreType.DMA
     shape = jax.ShapeDtypeStruct
-    master, first, second, turned, grads, frag, loss = pl.pallas_call(
+    master, first, second, turned, grads, loss = pl.pallas_call(
         functools.partial(window_kernel, n, replicas, dims),
         out_shape=[
             shape((rows, width), F32), shape((rows, width), F32), shape((rows, width), F32),
             shape((rows, everyone), BF16), shape((everyone, width), BF16),
-            shape((rows, fw), F32), shape((8, LANES), F32),
+            shape((8, LANES), F32),
         ],
-        in_specs=[any_spec, vmem, vmem, any_spec, any_spec, any_spec, any_spec, any_spec, smem],
-        out_specs=[any_spec] * 6 + [vmem],
+        in_specs=[any_spec, any_spec, any_spec, any_spec, any_spec, any_spec, any_spec, any_spec, smem],
+        out_specs=[any_spec] * 5 + [vmem],
         scratch_shapes=[
             pltpu.VMEM((steps, everyone, rows), BF16),
             pltpu.VMEM((steps, tokens, model), BF16),
+            pltpu.VMEM((1, steps, tokens, width), BF16),
+            pltpu.VMEM((1, steps, tokens), jnp.int32),
             pltpu.VMEM((rows, width), BF16),
             pltpu.VMEM((rows, width), BF16),
             pltpu.VMEM((rows, width), BF16),
@@ -371,14 +381,14 @@
             pltpu.VMEM((own, fw), BF16),
             pltpu.VMEM((steps, tokens, LANES), F32),
             pltpu.VMEM((steps, tokens, LANES), F32),
-            dma((6 + steps,)), dma((6,)),
+            dma((8 + steps,)), dma((5,)),
             dma((steps, n)), dma((steps, n)), dma((n,)), dma((n,)),
             dma((replicas,)), dma((replicas,)), dma((replicas,)), dma((replicas,)),
             dma((steps, n)), dma((steps, n)),
             dma((steps, n)), dma((steps, n)), dma((n,)), dma((n,)),
         ],
         compiler_params=pltpu.CompilerParams(
-            collective_id=0, has_side_effects=True, vmem_limit_bytes=52 * 1024 * 1024),
+            collective_id=0, has_side_effects=True, vmem_limit_bytes=60 * 1024 * 1024),
         name="window",
     )(hidden, targets, doc_ids, weights, adam_m, adam_v, anchor, momentum, fragment)
 
@@ -390,11 +400,11 @@
         grid=(rows // rt,),
         out_shape=[shape((1, rows, width), F32), shape((1, steps), F32)],
         in_specs=[smem, piece(width), piece(width), piece(width), piece(everyone),
-                  whole((everyone, width)), piece(fw), whole((8, LANES))],
+                  whole((everyone, width)), whole((8, LANES))],
         out_specs=[pl.BlockSpec((1, rt, width), lambda i: (0, i, 0)), whole((1, steps))],
-        compiler_params=pltpu.CompilerParams(vmem_limit_bytes=32 * 1024 * 1024),
+        compiler_params=pltpu.CompilerParams(vmem_limit_bytes=60 * 1024 * 1024),
         name="finish",
-    )(fragment, master, first, second, turned, grads, frag, loss)
+    )(fragment, master, first, second, turned, grads, loss)
 
 
 def solution(mesh):

time: 111 us -> 103 us (0.928)
  local copies, waits for them, and re-layouts: 12.7 us -> 0 us
  Pallas kernels: 96.3 us -> 101 us
    unnamed x18 -> x0, local copies, waits for them, and re-layouts: 12.7 us -> none
    pallas_call x1, Pallas kernels: 6.21 us -> 9.89 us  [body(): pl.pallas_call(functools.partial(finish_kernel, model ** (-0.5), fw), gri...]
    pallas_call x1, Pallas kernels: 90.1 us -> 91.4 us  [body(): pl.pallas_call(functools.partial(window_kernel, n, replicas, dims), out_s...]
where the time goes in v2:
time: 103 us
  Pallas kernels  101 us (98%)
  between operations  1.29 us (1%)
    pallas_call x1, Pallas kernels, body(): pl.pallas_call(functools.partial(window_kernel, n, replicas, dims), out_s...  91.4 us
    pallas_call x1, Pallas kernels, body(): pl.pallas_call(functools.partial(finish_kernel, model ** (-0.5), fw), gri...  9.89 us

profile of v2, /device:TPU:0, one launch (start us, length us, event | category | flops | bytes accessed | tf_op | source)
XLA Modules:
  0.0 102.5 jit_solution(643216499941330421)
XLA Ops:
  1.3 91.4 %window.1 = (f32[2048,512]{1,0:T(8,128)}, f32[2048,512]{1,0:T(8,128)}, f32[2048,512]{1,0:T(8,128)}, bf16[2048,256]{1,0:T(8,128)(2,1)}, bf16[256,512]{1,0:T(8,128)(2,1)}, /*index=5*/f32[8,128]{1,0:T(8,128)}) custom-call(bf16[1,2,64,8192]{3,2,1,0:T(8,128)(2,1)} %hidden.1, bf16[1,2,64,512]{3,2,1,0:T(8,128)(2,1)} %targets_in.1, s32[1,2,64]{2,1,0:T(2,128)} %ids_in.1, ...), custom_call_target="tpu_custom_call" | custom-call | tf_op jit(solution)/shard_map/window/pallas_call | solution.py:349
  92.6 9.9 %finish.1 = (f32[1,2048,512]{2,1,0:T(8,128)}, f32[1,2]{1,0:T(1,128)}) custom-call(s32[1]{0:T(128)S(6)} %copy.11.fragment, f32[2048,512]{1,0:T(8,128)} %get-tuple-element.8.kept, f32[2048,512]{1,0:T(8,128)} %get-tuple-element.9.first, f32[2048,512]{1,0:T(8,128)} %get-tuple-element.10.second, bf16[2048,256]{1,0:T(8,128)(2,1)} %get-tuple-element.11.turned, ...), custom_call_target="tpu_custom_call" | custom-call | tf_op jit(solution)/shard_map/finish/pallas_call | solution.py:398

commit v3 on v2

--- a/solution.py
+++ b/solution.py
@@ -39,11 +39,11 @@
 def window_kernel(
     n, replicas, dims,
     hidden, targets_in, ids_in, weights, adam_m, adam_v, anchor, momentum, fragment,
-    master_out, first_out, second_out, turned_out, grads_out, loss_out,
-    cols, hid, targets, doc_ids, w_ref, m_ref, v_ref, current, master, first, second, turned,
-    partial, part_send, part_recv, grads, counts, losses,
+    master, first, second, turned, grads, loss_out,
+    cols, hid, targets, doc_ids, w_ref, m_ref, v_ref, current,
+    partial, part_send, part_recv, counts, losses,
     frag_cols, frag_recv, frag_all, anchor_ref, moment_ref, row_scale, token_weight,
-    local_sem, out_sem, a2a_send, a2a_recv, count_send, count_recv,
+    local_sem, a2a_send, a2a_recv, count_send, count_recv,
     frag_send, frag_got, all_send, all_got, part_send_sem, part_recv_sem,
     grad_send, grad_recv, loss_send, loss_recv,
 ):
@@ -283,19 +283,7 @@
             piece = kept[:, k * fw:(k + 1) * fw]
             master[at, k * fw:(k + 1) * fw] = jnp.where(picked == k, MIXING * piece + mixed, piece)
 
-    outs = [
-        pltpu.make_async_copy(master, master_out, out_sem.at[0]),
-        pltpu.make_async_copy(first, first_out, out_sem.at[1]),
-        pltpu.make_async_copy(second, second_out, out_sem.at[2]),
-    ]
-    for copy in outs:
-        copy.start()
-
     project_and_share(1, current)
-    outs.append(pltpu.make_async_copy(turned.at[1], turned_out, out_sem.at[3]))
-    outs.append(pltpu.make_async_copy(grads.at[1], grads_out, out_sem.at[4]))
-    outs[-2].start()
-    outs[-1].start()
     for j in others:
         from_all(losses, loss_send, loss_recv, j)
     loss = losses[0]
@@ -313,25 +301,41 @@
     for i in peers:
         frag_copy(i).wait_send()
         all_copy(i).wait_send()
-    for copy in outs:
-        copy.wait()
-
-
-def finish_kernel(scale, fw, fragment, kept, first, second, turned, grads, loss, out, loss_out):
-    raw = jnp.dot(turned[...], grads[...], preferred_element_type=F32)
-    moved = first[...] + (INNER_RATE * (1.0 - BETA_FIRST) * scale) * raw
-    power = second[...] + ((1.0 - BETA_SECOND) * scale * scale) * (raw * raw)
-    step = moved / (power * lax.rsqrt(power) + ADAM_EPS)
-    width = out.shape[2]
+
+
+def finish_kernel(scale, fw, fragment, kept, first, second, turned, grads, loss, out, loss_out,
+                  done, out_sem):
+    rows, width = kept.shape
+    last = turned.shape[0] - 1
+    tiles = out_sem.shape[0]
+    rt = rows // tiles
     column = lax.broadcasted_iota(jnp.int32, (1, width), 1) // fw
     share = jnp.where(column == fragment[0], MIXING, 1.0)
-    out[0] = kept[...] - share * step
+
+    def write(c):
+        at = pl.ds(pl.multiple_of(c * rt, rt), rt)
+        return pltpu.make_async_copy(done.at[at, :], out.at[0, at, :], out_sem.at[c])
+
+    @pl.loop(0, tiles)
+    def _(c):
+        at = pl.ds(pl.multiple_of(c * rt, rt), rt)
+        raw = jnp.dot(turned[last, at, :], grads[last], preferred_element_type=F32)
+        moved = first[at, :] + (INNER_RATE * (1.0 - BETA_FIRST) * scale) * raw
+        power = second[at, :] + ((1.0 - BETA_SECOND) * scale * scale) * (raw * raw)
+        step = moved / (power * lax.rsqrt(power) + ADAM_EPS)
+        done[at, :] = kept[at, :] - share * step
+        write(c).start()
+
     steps = loss_out.shape[1]
     across = lax.broadcasted_iota(jnp.int32, (1, steps), 1)
     line = jnp.zeros((1, steps), F32)
     for s in range(steps):
         line = jnp.where(across == s, loss[s:s + 1, :steps], line)
     loss_out[...] = line
+
+    @pl.loop(0, tiles)
+    def _(c):
+        write(c).wait()
 
 
 def body(n, replicas, hidden, targets, doc_ids, weights, adam_m, adam_v, anchor, momentum, fragment):
@@ -346,15 +350,17 @@
     smem = pl.BlockSpec(memory_space=pltpu.SMEM)
     dma = pltpu.SemaphoreType.DMA
     shape = jax.ShapeDtypeStruct
+    outer = [pltpu.with_memory_space_constraint(x, pltpu.HBM) for x in (
+        hidden, targets, doc_ids, weights, adam_m, adam_v, anchor, momentum)]
     master, first, second, turned, grads, loss = pl.pallas_call(
         functools.partial(window_kernel, n, replicas, dims),
         out_shape=[
-            shape((rows, width), F32), shape((rows, width), F32), shape((rows, width), F32),
-            shape((rows, everyone), BF16), shape((everyone, width), BF16),
-            shape((8, LANES), F32),
+            pltpu.VMEM((rows, width), F32), pltpu.VMEM((rows, width), F32),
+            pltpu.VMEM((rows, width), F32), pltpu.VMEM((steps, rows, everyone), BF16),
+            pltpu.VMEM((steps, everyone, width), BF16), pltpu.VMEM((8, LANES), F32),
         ],
-        in_specs=[any_spec, any_spec, any_spec, any_spec, any_spec, any_spec, any_spec, any_spec, smem],
-        out_specs=[any_spec] * 5 + [vmem],
+        in_specs=[any_spec] * 8 + [smem],
+        out_specs=[vmem] * 6,
         scratch_shapes=[
             pltpu.VMEM((steps, everyone, rows), BF16),
             pltpu.VMEM((steps, tokens, model), BF16),
@@ -364,14 +370,9 @@
             pltpu.VMEM((rows, width), BF16),
             pltpu.VMEM((rows, width), BF16),
             pltpu.VMEM((rows, width), BF16),
-            pltpu.VMEM((rows, width), F32),
-            pltpu.VMEM((rows, width), F32),
-            pltpu.VMEM((rows, width), F32),
-            pltpu.VMEM((steps, rows, everyone), BF16),
             pltpu.VMEM((everyone, width), F32),
             pltpu.VMEM((steps, everyone, width), BF16),
             pltpu.VMEM((steps, n, tokens, width), BF16),
-            pltpu.VMEM((steps, everyone, width), BF16),
             pltpu.VMEM((n, 8, LANES), F32),
             pltpu.VMEM((n, 8, LANES), F32),
             pltpu.VMEM((rows, fw), BF16),
@@ -381,30 +382,28 @@
             pltpu.VMEM((own, fw), BF16),
             pltpu.VMEM((steps, tokens, LANES), F32),
             pltpu.VMEM((steps, tokens, LANES), F32),
-            dma((8 + steps,)), dma((5,)),
+            dma((8 + steps,)),
             dma((steps, n)), dma((steps, n)), dma((n,)), dma((n,)),
             dma((replicas,)), dma((replicas,)), dma((replicas,)), dma((replicas,)),
             dma((steps, n)), dma((steps, n)),
             dma((steps, n)), dma((steps, n)), dma((n,)), dma((n,)),
         ],
         compiler_params=pltpu.CompilerParams(
-            collective_id=0, has_side_effects=True, vmem_limit_bytes=60 * 1024 * 1024),
+            collective_id=0, has_side_effects=True, vmem_limit_bytes=28 * 1024 * 1024),
         name="window",
-    )(hidden, targets, doc_ids, weights, adam_m, adam_v, anchor, momentum, fragment)
-
-    rt = min(256, rows)
-    whole = lambda shape: pl.BlockSpec(shape, lambda i: (0, 0))
-    piece = lambda cols: pl.BlockSpec((rt, cols), lambda i: (i, 0))
+    )(*outer, fragment)
+
+    inner = [pltpu.with_memory_space_constraint(x, pltpu.VMEM)
+             for x in (master, first, second, turned, grads, loss)]
     return pl.pallas_call(
         functools.partial(finish_kernel, model ** (-0.5), fw),
-        grid=(rows // rt,),
         out_shape=[shape((1, rows, width), F32), shape((1, steps), F32)],
-        in_specs=[smem, piece(width), piece(width), piece(width), piece(everyone),
-                  whole((everyone, width)), whole((8, LANES))],
-        out_specs=[pl.BlockSpec((1, rt, width), lambda i: (0, i, 0)), whole((1, steps))],
-        compiler_params=pltpu.CompilerParams(vmem_limit_bytes=60 * 1024 * 1024),
+        in_specs=[smem] + [vmem] * 6,
+        out_specs=[any_spec, vmem],
+        scratch_shapes=[pltpu.VMEM((rows, width), F32), dma((8,))],
+        compiler_params=pltpu.CompilerParams(vmem_limit_bytes=16 * 1024 * 1024),
         name="finish",
-    )(fragment, master, first, second, turned, grads, loss)
+    )(fragment, *inner)
 
 
 def solution(mesh):

time: 103 us -> 96.7 us (0.939)
  Pallas kernels: 101 us -> 95.2 us
    pallas_call x1, Pallas kernels: 9.89 us -> 4.42 us  [body(): pl.pallas_call(functools.partial(finish_kernel, model ** (-0.5), fw), out...]
where the time goes in v3:
time: 96.7 us; the launch traced here: 96.5 us
  Pallas kernels  95.2 us (98%)
  between operations  1.29 us (1%)
    pallas_call x1, Pallas kernels, body(): pl.pallas_call(functools.partial(window_kernel, n, replicas, dims), out_s...  90.8 us
    pallas_call x1, Pallas kernels, body(): pl.pallas_call(functools.partial(finish_kernel, model ** (-0.5), fw), out...  4.42 us

profile of v3, /device:TPU:0, one launch (start us, length us, event | category | flops | bytes accessed | tf_op | source)
XLA Modules:
  0.0 96.5 jit_solution(913504213430281156)
XLA Ops:
  1.3 90.8 %window.1 = (f32[2048,512]{1,0:T(8,128)S(1)}, f32[2048,512]{1,0:T(8,128)S(1)}, f32[2048,512]{1,0:T(8,128)S(1)}, bf16[2,2048,256]{2,1,0:T(8,128)(2,1)S(1)}, bf16[...) custom-call(bf16[1,2,64,8192]{3,2,1,0:T(8,128)(2,1)} %hidden.1, bf16[1,2,64,512]{3,2,1,0:T(8,128)(2,1)} %targets_in.1, ...), custom_call_target="tpu_custom_call" | custom-call | tf_op jit(solution)/shard_map/window/pallas_call | solution.py:355
  92.1 4.4 %finish.1 = (f32[1,2048,512]{2,1,0:T(8,128)}, f32[1,2]{1,0:T(1,128)}) custom-call(s32[1]{0:T(128)S(6)} %copy.11.fragment, f32[2048,512]{1,0:T(8,128)S(1)} %get-tuple-element.8.kept, f32[2048,512]{1,0:T(8,128)S(1)} %get-tuple-element.9.first, f32[2048,512]{1,0:T(8,128)S(1)} %get-tuple-element.10.second, bf16[2,2048,256]{2,1,0:T(8,128)(2,1)S(1)} %get-tuple-element.11.turned, ...), custom_call_target="tpu_custom_call" | custom-call | tf_op jit(solution)/shard_map/finish/pallas_call | solution.py:398

commit v4 on v3

--- a/solution.py
+++ b/solution.py
@@ -43,11 +43,17 @@
     cols, hid, targets, doc_ids, w_ref, m_ref, v_ref, current,
     partial, part_send, part_recv, counts, losses,
     frag_cols, frag_recv, frag_all, anchor_ref, moment_ref, row_scale, token_weight,
+    coef_mine, coef_got, coef_across, coef_sem,
     local_sem, a2a_send, a2a_recv, count_send, count_recv,
     frag_send, frag_got, all_send, all_got, part_send_sem, part_recv_sem,
     grad_send, grad_recv, loss_send, loss_recv,
 ):
     steps, tokens, rows, width, model, fw = dims
+    paired = n == 4 and tokens <= LANES
+    units = cols.shape[0]
+    parts = units // steps
+    few = tokens // parts
+    together = n * few
     own = rows // replicas
     scale = model ** (-0.5)
     rep = lax.axis_index("replica")
@@ -58,7 +64,10 @@
     def block(index, size):
         return pl.ds(pl.multiple_of(index * size, size), size)
 
-    my_tokens = block(me, tokens)
+    def slot(j):
+        return 2 * lax.rem(j, 2) + j // 2 if paired else j
+
+    my_tokens = block(slot(me), few)
     my_frag = block(rep, own)
 
     local = [
@@ -69,11 +78,15 @@
         pltpu.make_async_copy(adam_m.at[0], m_ref, local_sem.at[4]),
         pltpu.make_async_copy(adam_v.at[0], v_ref, local_sem.at[5]),
     ]
-    for s in range(steps):
+
+    def held_tokens(u, j):
+        return hidden.at[0, u // parts, u % parts * few:(u % parts + 1) * few, block(j, rows)]
+
+    for u in range(units):
         local.append(pltpu.make_async_copy(
-            hidden.at[0, s, :, block(me, rows)], cols.at[s, my_tokens, :], local_sem.at[6 + s]))
-    local.append(pltpu.make_async_copy(targets_in, targets, local_sem.at[6 + steps]))
-    local.append(pltpu.make_async_copy(ids_in, doc_ids, local_sem.at[7 + steps]))
+            held_tokens(u, me), cols.at[u, my_tokens, :], local_sem.at[6 + u]))
+    local.append(pltpu.make_async_copy(targets_in, targets, local_sem.at[6 + units]))
+    local.append(pltpu.make_async_copy(ids_in, doc_ids, local_sem.at[7 + units]))
     for copy in local:
         copy.start()
 
@@ -84,25 +97,28 @@
         pl.semaphore_signal(barrier, inc=1, device_id=(i, me), device_id_type=MESH)
     pl.semaphore_wait(barrier, n + replicas - 2)
 
-    def a2a(s, j):
-        return pltpu.make_async_remote_copy(
-            src_ref=hidden.at[0, s, :, block(j, rows)], dst_ref=cols.at[s, my_tokens, :],
-            send_sem=a2a_send.at[s, j], recv_sem=a2a_recv.at[s, me],
+    def a2a(u, j):
+        return pltpu.make_async_remote_copy(
+            src_ref=held_tokens(u, j), dst_ref=cols.at[u, my_tokens, :],
+            send_sem=a2a_send.at[u, j], recv_sem=a2a_recv.at[u, me],
             device_id=(rep, j), device_id_type=MESH)
 
-    def a2a_arrived(s, j):
+    def a2a_arrived(u, j):
         pltpu.make_async_remote_copy(
-            src_ref=hidden.at[0, s, :, block(j, rows)], dst_ref=cols.at[s, block(j, tokens), :],
-            send_sem=a2a_send.at[s, j], recv_sem=a2a_recv.at[s, j],
+            src_ref=held_tokens(u, j), dst_ref=cols.at[u, block(slot(j), few), :],
+            send_sem=a2a_send.at[u, j], recv_sem=a2a_recv.at[u, j],
             device_id=(rep, j), device_id_type=MESH).wait_recv()
 
-    for j in others:
-        a2a(0, j).start()
-
-    local[7 + steps].wait()
+    for u in range(min(2, units)):
+        for j in others:
+            a2a(u, j).start()
+
+    local[7 + units].wait()
     lane = lax.broadcasted_iota(jnp.int32, (tokens, LANES), 1).astype(F32)
     eye = (lax.broadcasted_iota(jnp.int32, (tokens, tokens), 0)
            == lax.broadcasted_iota(jnp.int32, (tokens, tokens), 1))
+    wide_eye = (lax.broadcasted_iota(jnp.int32, (tokens, LANES), 0)
+                == lax.broadcasted_iota(jnp.int32, (tokens, LANES), 1))
     onehots = []
     row8 = lax.broadcasted_iota(jnp.int32, (8, LANES), 0)
     tally = jnp.zeros((8, LANES), F32)
@@ -165,6 +181,20 @@
     for s in range(steps):
         weight = jnp.sum(onehots[s] * inverse[s:s + 1, :], axis=1, keepdims=True)
         token_weight[s] = jnp.broadcast_to(weight, (tokens, LANES))
+
+    def across():
+        return pltpu.make_async_remote_copy(
+            src_ref=coef_mine, dst_ref=coef_got, send_sem=coef_sem.at[0], recv_sem=coef_sem.at[1],
+            device_id=(rep, lax.rem(me + 2, n)), device_id_type=MESH)
+
+    if paired:
+        lines = jnp.zeros((8, LANES), F32)
+        for s in range(steps):
+            coef = token_weight[s] * row_scale[s] * row_scale[s] * (scale / width)
+            line = jnp.sum(jnp.where(wide_eye, coef, 0.0), axis=0, keepdims=True)
+            lines = lines + jnp.where(row8 == s, line, 0.0)
+        coef_mine[...] = lines
+        across().start()
 
     for i in peers:
         pltpu.make_async_remote_copy(
@@ -189,75 +219,144 @@
     for i in peers:
         all_copy(i).start()
 
-    local[6 + steps].wait()
-
-    for j in others:
-        a2a(0, j).wait_send()
-        a2a(1, j).start()
-
-    def part_copy(s, j):
-        return pltpu.make_async_remote_copy(
-            src_ref=part_send.at[s, block(j, tokens), :], dst_ref=part_recv.at[s, me],
-            send_sem=part_send_sem.at[s, j], recv_sem=part_recv_sem.at[s, me],
+    local[6 + units].wait()
+
+    if paired:
+        across().wait_recv()
+        for s in range(steps):
+            line = jnp.broadcast_to(coef_got[s:s + 1, :], (tokens, LANES))
+            column = jnp.sum(jnp.where(wide_eye, line, 0.0), axis=1, keepdims=True)
+            coef_across[s] = jnp.broadcast_to(column, (tokens, LANES))
+
+    def part_copy(u, j):
+        return pltpu.make_async_remote_copy(
+            src_ref=part_send.at[u, block(j, few), :], dst_ref=part_recv.at[u, my_tokens, :],
+            send_sem=part_send_sem.at[u, j], recv_sem=part_recv_sem.at[u, me],
             device_id=(rep, j), device_id_type=MESH)
 
-    def grad_copy(s, j):
-        return pltpu.make_async_remote_copy(
-            src_ref=grads.at[s, my_tokens, :], dst_ref=grads.at[s, my_tokens, :],
-            send_sem=grad_send.at[s, j], recv_sem=grad_recv.at[s, me],
-            device_id=(rep, j), device_id_type=MESH)
+    def grad_rows(u, first_row, size):
+        start = u % parts * together + first_row * size
+        return grads.at[u // parts, pl.ds(pl.multiple_of(start, size), size), :]
+
+    def grad_copy(u, j):
+        mine = grad_rows(u, me, few)
+        return pltpu.make_async_remote_copy(
+            src_ref=mine, dst_ref=mine, send_sem=grad_send.at[u, j],
+            recv_sem=grad_recv.at[u, me], device_id=(rep, j), device_id_type=MESH)
+
+    side, half = lax.rem(me, 2), me // 2
+    mate, cross = me + 1 - 2 * side, lax.rem(me + 2, n)
+    my_side, mate_side = block(side, 2 * few), block(1 - side, 2 * few)
+
+    def pair_copy(kind, u):
+        if kind == 0:
+            src, dst, to = part_send.at[u, mate_side, :], part_recv.at[u, 0:2 * few, :], mate
+        elif kind == 1:
+            src, dst, to = part_send.at[u, my_side, :], part_recv.at[u, 2 * few:4 * few, :], cross
+        else:
+            src = dst = grad_rows(u, side, 2 * few)
+            to = mate
+        return pltpu.make_async_remote_copy(
+            src_ref=src, dst_ref=dst, send_sem=part_send_sem.at[u, kind],
+            recv_sem=part_recv_sem.at[u, kind], device_id=(rep, to), device_id_type=MESH)
+
+    def pair_back(u):
+        theirs = grad_rows(u, 1 - side, 2 * few)
+        pltpu.make_async_remote_copy(
+            src_ref=theirs, dst_ref=theirs, send_sem=part_send_sem.at[u, 2],
+            recv_sem=part_recv_sem.at[u, 2], device_id=(rep, mate),
+            device_id_type=MESH).wait_recv()
 
     tile = 256
 
-    def project_and_share(s, held):
+    def project_and_share(u, held):
+        s, q = u // parts, u % parts
         for j in others:
-            a2a_arrived(s, j)
-        local[6 + s].wait()
+            a2a_arrived(u, j)
+        local[6 + u].wait()
 
         @pl.loop(0, width // tile)
         def _(c):
             at = block(c, tile)
-            out = jnp.dot(cols[s], held[:, at], preferred_element_type=F32)
+            out = jnp.dot(cols[u], held[:, at], preferred_element_type=F32)
             partial[:, at] = out
-            part_send[s, :, at] = out.astype(BF16)
-
-        for j in others:
-            part_copy(s, j).start()
+            part_send[u, :, at] = out.astype(BF16)
+
+        if paired:
+            pair_copy(0, u).start()
+        else:
+            for j in others:
+                part_copy(u, j).start()
 
         @pl.loop(0, rows // tile)
         def _(c):
             at = block(c, tile)
-            turned[s, at, :] = cols[s, :, at].T
-
-        values = partial[my_tokens, :]
-        for j in others:
-            pltpu.make_async_remote_copy(
-                src_ref=part_recv.at[s, j], dst_ref=part_recv.at[s, j],
-                send_sem=part_send_sem.at[s, j], recv_sem=part_recv_sem.at[s, j],
-                device_id=(rep, j), device_id_type=MESH).wait_recv()
-            values = values + part_recv[s, j].astype(F32)
-        gain = row_scale[s][:, :1]
-        weight = token_weight[s][:, :1]
-        error = values * (gain * scale) - targets[0, s].astype(F32)
-        grads[s, my_tokens, :] = ((weight * gain / width) * error).astype(BF16)
-        for j in others:
-            grad_copy(s, j).start()
+            turned[s, at, q * together:(q + 1) * together] = cols[u, :, at].T
+
+        few_rows = slice(q * few, (q + 1) * few)
+        gain = row_scale[s, few_rows, :][:, :1]
+        weight = token_weight[s, few_rows, :][:, :1]
+        goal = targets[0, s, few_rows, :].astype(F32)
+        if paired:
+            share = weight * gain / width
+            mine, theirs = block(half, few), block(1 - half, few)
+            pair_copy(0, u).wait_recv()
+            near = (partial[my_tokens, :] + part_recv[u, mine, :].astype(F32)) * (share * gain * scale)
+            near = near - share * goal
+            far = partial[block(slot(cross), few), :] + part_recv[u, theirs, :].astype(F32)
+            far = far * coef_across[s, few_rows, :][:, :1]
+            part_send[u, my_tokens, :] = near.astype(BF16)
+            part_send[u, block(slot(cross), few), :] = far.astype(BF16)
+            pair_copy(1, u).start()
+            pair_copy(1, u).wait_recv()
+            base = 2 * few
+            near = near + part_recv[u, pl.ds(pl.multiple_of(base + half * few, few), few), :].astype(F32)
+            far = far + part_recv[u, pl.ds(pl.multiple_of(base + (1 - half) * few, few), few), :].astype(F32)
+            start = q * together
+            grads[s, pl.ds(pl.multiple_of(start + slot(me) * few, few), few), :] = near.astype(BF16)
+            grads[s, pl.ds(pl.multiple_of(start + slot(cross) * few, few), few), :] = far.astype(BF16)
+            pair_copy(2, u).start()
+            error = near / share
+        else:
+            values = partial[my_tokens, :]
+            for j in others:
+                at = block(j, few)
+                pltpu.make_async_remote_copy(
+                    src_ref=part_recv.at[u, at, :], dst_ref=part_recv.at[u, at, :],
+                    send_sem=part_send_sem.at[u, j], recv_sem=part_recv_sem.at[u, j],
+                    device_id=(rep, j), device_id_type=MESH).wait_recv()
+                values = values + part_recv[u, at, :].astype(F32)
+            error = values * (gain * scale) - goal
+            start = q * together + me * few
+            grads[s, pl.ds(pl.multiple_of(start, few), few), :] = (
+                (weight * gain / width) * error).astype(BF16)
+            for j in others:
+                grad_copy(u, j).start()
         loss = jnp.sum(weight * 0.5 * jnp.mean(error * error, axis=-1, keepdims=True))
         loss = jnp.where(row8 == s, loss, 0.0)
-        if s == 0:
+        if u == 0:
             losses[me] = loss
         else:
             losses[me] = losses[me] + loss
-        if s == steps - 1:
+        if u == units - 1:
             for j in others:
                 to_all(losses, loss_send, loss_recv, j).start()
+        if paired:
+            pair_back(u)
+        else:
+            for j in others:
+                theirs = grad_rows(u, j, few)
+                pltpu.make_async_remote_copy(
+                    src_ref=theirs, dst_ref=theirs, send_sem=grad_send.at[u, j],
+                    recv_sem=grad_recv.at[u, j], device_id=(rep, j),
+                    device_id_type=MESH).wait_recv()
+
+    for u in range(parts):
         for j in others:
-            pltpu.make_async_remote_copy(
-                src_ref=grads.at[s, block(j, tokens), :], dst_ref=grads.at[s, block(j, tokens), :],
-                send_sem=grad_send.at[s, j], recv_sem=grad_recv.at[s, j],
-                device_id=(rep, j), device_id_type=MESH).wait_recv()
-
-    project_and_share(0, w_ref)
+            a2a(u, j).wait_send()
+            if u + 2 < units:
+                a2a(u + 2, j).start()
+        project_and_share(u, w_ref)
     local[4].wait()
     local[5].wait()
     rt = 128
@@ -283,7 +382,12 @@
             piece = kept[:, k * fw:(k + 1) * fw]
             master[at, k * fw:(k + 1) * fw] = jnp.where(picked == k, MIXING * piece + mixed, piece)
 
-    project_and_share(1, current)
+    for u in range(parts, units):
+        if u + 2 < units:
+            for j in others:
+                a2a(u, j).wait_send()
+                a2a(u + 2, j).start()
+        project_and_share(u, current)
     for j in others:
         from_all(losses, loss_send, loss_recv, j)
     loss = losses[0]
@@ -292,12 +396,20 @@
     loss_out[...] = loss
 
     for j in others:
-        a2a(1, j).wait_send()
+        for u in range(parts, units):
+            if u + 2 >= units:
+                a2a(u, j).wait_send()
         to_all(counts, count_send, count_recv, j).wait_send()
         to_all(losses, loss_send, loss_recv, j).wait_send()
-        for s in range(steps):
-            part_copy(s, j).wait_send()
-            grad_copy(s, j).wait_send()
+        if not paired:
+            for u in range(units):
+                part_copy(u, j).wait_send()
+                grad_copy(u, j).wait_send()
+    if paired:
+        across().wait_send()
+        for u in range(units):
+            for kind in range(3):
+                pair_copy(kind, u).wait_send()
     for i in peers:
         frag_copy(i).wait_send()
         all_copy(i).wait_send()
@@ -344,6 +456,9 @@
     fw = anchor.shape[1]
     own = rows // replicas
     everyone = n * tokens
+    parts = 2 if tokens % 32 == 0 else 1
+    units = steps * parts
+    together = everyone // parts
     dims = (steps, tokens, rows, width, model, fw)
     any_spec = pl.BlockSpec(memory_space=pltpu.HBM)
     vmem = pl.BlockSpec(memory_space=pltpu.VMEM)
@@ -362,7 +477,7 @@
         in_specs=[any_spec] * 8 + [smem],
         out_specs=[vmem] * 6,
         scratch_shapes=[
-            pltpu.VMEM((steps, everyone, rows), BF16),
+            pltpu.VMEM((units, together, rows), BF16),
             pltpu.VMEM((steps, tokens, model), BF16),
             pltpu.VMEM((1, steps, tokens, width), BF16),
             pltpu.VMEM((1, steps, tokens), jnp.int32),
@@ -370,9 +485,9 @@
             pltpu.VMEM((rows, width), BF16),
             pltpu.VMEM((rows, width), BF16),
             pltpu.VMEM((rows, width), BF16),
-            pltpu.VMEM((everyone, width), F32),
-            pltpu.VMEM((steps, everyone, width), BF16),
-            pltpu.VMEM((steps, n, tokens, width), BF16),
+            pltpu.VMEM((together, width), F32),
+            pltpu.VMEM((units, together, width), BF16),
+            pltpu.VMEM((units, together, width), BF16),
             pltpu.VMEM((n, 8, LANES), F32),
             pltpu.VMEM((n, 8, LANES), F32),
             pltpu.VMEM((rows, fw), BF16),
@@ -382,11 +497,15 @@
             pltpu.VMEM((own, fw), BF16),
             pltpu.VMEM((steps, tokens, LANES), F32),
             pltpu.VMEM((steps, tokens, LANES), F32),
-            dma((8 + steps,)),
-            dma((steps, n)), dma((steps, n)), dma((n,)), dma((n,)),
+            pltpu.VMEM((8, LANES), F32),
+            pltpu.VMEM((8, LANES), F32),
+            pltpu.VMEM((steps, tokens, LANES), F32),
+            dma((2,)),
+            dma((8 + units,)),
+            dma((units, n)), dma((units, n)), dma((n,)), dma((n,)),
             dma((replicas,)), dma((replicas,)), dma((replicas,)), dma((replicas,)),
-            dma((steps, n)), dma((steps, n)),
-            dma((steps, n)), dma((steps, n)), dma((n,)), dma((n,)),
+            dma((units, n)), dma((units, n)),
+            dma((units, n)), dma((units, n)), dma((n,)), dma((n,)),
         ],
         compiler_params=pltpu.CompilerParams(
             collective_id=0, has_side_effects=True, vmem_limit_bytes=28 * 1024 * 1024),

time: 96.7 us -> 106 us (1.096)
  Pallas kernels: 95.2 us -> 105 us
    pallas_call x1, Pallas kernels: 90.8 us -> 100 us  [body(): pl.pallas_call(functools.partial(window_kernel, n, replicas, dims), out_s...]
where the time goes in v4:
time: 106 us
  Pallas kernels  105 us (99%)
  between operations  1.29 us (1%)
    pallas_call x1, Pallas kernels, body(): pl.pallas_call(functools.partial(window_kernel, n, replicas, dims), out_s...  100 us
    pallas_call x1, Pallas kernels, body(): pl.pallas_call(functools.partial(finish_kernel, model ** (-0.5), fw), out...  4.42 us

profile of v4, /device:TPU:0, one launch (start us, length us, event | category | flops | bytes accessed | tf_op | source)
XLA Modules:
  0.0 105.9 jit_solution(11612054517266937605)
XLA Ops:
  1.3 100.2 %window.1 = (f32[2048,512]{1,0:T(8,128)S(1)}, f32[2048,512]{1,0:T(8,128)S(1)}, f32[2048,512]{1,0:T(8,128)S(1)}, bf16[2,2048,256]{2,1,0:T(8,128)(2,1)S(1)}, bf16[...) custom-call(bf16[1,2,64,8192]{3,2,1,0:T(8,128)(2,1)} %hidden.1, bf16[1,2,64,512]{3,2,1,0:T(8,128)(2,1)} %targets_in.1, ...), custom_call_target="tpu_custom_call" | custom-call | tf_op jit(solution)/shard_map/window/pallas_call | solution.py:470
  101.4 4.4 %finish.1 = (f32[1,2048,512]{2,1,0:T(8,128)}, f32[1,2]{1,0:T(1,128)}) custom-call(s32[1]{0:T(128)S(6)} %copy.11.fragment, f32[2048,512]{1,0:T(8,128)S(1)} %get-tuple-element.8.kept, f32[2048,512]{1,0:T(8,128)S(1)} %get-tuple-element.9.first, f32[2048,512]{1,0:T(8,128)S(1)} %get-tuple-element.10.second, bf16[2,2048,256]{2,1,0:T(8,128)(2,1)S(1)} %get-tuple-element.11.turned, ...), custom_call_target="tpu_custom_call" | custom-call | tf_op jit(solution)/shard_map/finish/pallas_call | solution.py:517

commit v5 on v4

--- a/solution.py
+++ b/solution.py
@@ -109,7 +109,7 @@
             send_sem=a2a_send.at[u, j], recv_sem=a2a_recv.at[u, j],
             device_id=(rep, j), device_id_type=MESH).wait_recv()
 
-    for u in range(min(2, units)):
+    for u in range(parts):
         for j in others:
             a2a(u, j).start()
 
@@ -269,7 +269,14 @@
 
     tile = 256
 
-    def project_and_share(u, held):
+    def factors(u):
+        s, q = u // parts, u % parts
+        few_rows = slice(q * few, (q + 1) * few)
+        gain = row_scale[s, few_rows, :][:, :1]
+        weight = token_weight[s, few_rows, :][:, :1]
+        return s, q, few_rows, gain, weight
+
+    def project(u, held):
         s, q = u // parts, u % parts
         for j in others:
             a2a_arrived(u, j)
@@ -279,7 +286,7 @@
         def _(c):
             at = block(c, tile)
             out = jnp.dot(cols[u], held[:, at], preferred_element_type=F32)
-            partial[:, at] = out
+            partial[u, :, at] = out
             part_send[u, :, at] = out.astype(BF16)
 
         if paired:
@@ -293,32 +300,43 @@
             at = block(c, tile)
             turned[s, at, q * together:(q + 1) * together] = cols[u, :, at].T
 
-        few_rows = slice(q * few, (q + 1) * few)
-        gain = row_scale[s, few_rows, :][:, :1]
-        weight = token_weight[s, few_rows, :][:, :1]
+    def join_mate(u):
+        if not paired:
+            return
+        s, q, few_rows, gain, weight = factors(u)
+        share = weight * gain / width
         goal = targets[0, s, few_rows, :].astype(F32)
+        mine, theirs = block(half, few), block(1 - half, few)
+        other_rows = block(slot(cross), few)
+        pair_copy(0, u).wait_recv()
+        near = partial[u, my_tokens, :] + part_recv[u, mine, :].astype(F32)
+        near = near * (share * gain * scale) - share * goal
+        far = partial[u, other_rows, :] + part_recv[u, theirs, :].astype(F32)
+        far = far * coef_across[s, few_rows, :][:, :1]
+        part_send[u, my_tokens, :] = near.astype(BF16)
+        part_send[u, other_rows, :] = far.astype(BF16)
+        pair_copy(1, u).start()
+        partial[u, my_tokens, :] = near
+        partial[u, other_rows, :] = far
+
+    def join_across(u):
+        s, q, few_rows, gain, weight = factors(u)
+        start = q * together
         if paired:
             share = weight * gain / width
-            mine, theirs = block(half, few), block(1 - half, few)
-            pair_copy(0, u).wait_recv()
-            near = (partial[my_tokens, :] + part_recv[u, mine, :].astype(F32)) * (share * gain * scale)
-            near = near - share * goal
-            far = partial[block(slot(cross), few), :] + part_recv[u, theirs, :].astype(F32)
-            far = far * coef_across[s, few_rows, :][:, :1]
-            part_send[u, my_tokens, :] = near.astype(BF16)
-            part_send[u, block(slot(cross), few), :] = far.astype(BF16)
-            pair_copy(1, u).start()
+            other_rows = block(slot(cross), few)
+            base = 2 * few
             pair_copy(1, u).wait_recv()
-            base = 2 * few
-            near = near + part_recv[u, pl.ds(pl.multiple_of(base + half * few, few), few), :].astype(F32)
-            far = far + part_recv[u, pl.ds(pl.multiple_of(base + (1 - half) * few, few), few), :].astype(F32)
-            start = q * together
+            near = partial[u, my_tokens, :] + part_recv[
+                u, pl.ds(pl.multiple_of(base + half * few, few), few), :].astype(F32)
+            far = partial[u, other_rows, :] + part_recv[
+                u, pl.ds(pl.multiple_of(base + (1 - half) * few, few), few), :].astype(F32)
             grads[s, pl.ds(pl.multiple_of(start + slot(me) * few, few), few), :] = near.astype(BF16)
             grads[s, pl.ds(pl.multiple_of(start + slot(cross) * few, few), few), :] = far.astype(BF16)
             pair_copy(2, u).start()
             error = near / share
         else:
-            values = partial[my_tokens, :]
+            values = partial[u, my_tokens, :]
             for j in others:
                 at = block(j, few)
                 pltpu.make_async_remote_copy(
@@ -326,9 +344,8 @@
                     send_sem=part_send_sem.at[u, j], recv_sem=part_recv_sem.at[u, j],
                     device_id=(rep, j), device_id_type=MESH).wait_recv()
                 values = values + part_recv[u, at, :].astype(F32)
-            error = values * (gain * scale) - goal
-            start = q * together + me * few
-            grads[s, pl.ds(pl.multiple_of(start, few), few), :] = (
+            error = values * (gain * scale) - targets[0, s, few_rows, :].astype(F32)
+            grads[s, pl.ds(pl.multiple_of(start + me * few, few), few), :] = (
                 (weight * gain / width) * error).astype(BF16)
             for j in others:
                 grad_copy(u, j).start()
@@ -341,6 +358,8 @@
         if u == units - 1:
             for j in others:
                 to_all(losses, loss_send, loss_recv, j).start()
+
+    def join_all(u):
         if paired:
             pair_back(u)
         else:
@@ -351,12 +370,23 @@
                     recv_sem=grad_recv.at[u, j], device_id=(rep, j),
                     device_id_type=MESH).wait_recv()
 
-    for u in range(parts):
-        for j in others:
+    now, later = range(parts), range(parts, units)
+    queue = [(u, j) for u in later for j in others]
+    for j in others:
+        for u in now:
             a2a(u, j).wait_send()
-            if u + 2 < units:
-                a2a(u + 2, j).start()
-        project_and_share(u, w_ref)
+    a2a(*queue[0]).start()
+    for u in now:
+        project(u, w_ref)
+    for u in now:
+        join_mate(u)
+    a2a(*queue[1]).start()
+    for u in now:
+        join_across(u)
+    for u, j in queue[2:]:
+        a2a(u, j).start()
+    for u in now:
+        join_all(u)
     local[4].wait()
     local[5].wait()
     rt = 128
@@ -382,12 +412,11 @@
             piece = kept[:, k * fw:(k + 1) * fw]
             master[at, k * fw:(k + 1) * fw] = jnp.where(picked == k, MIXING * piece + mixed, piece)
 
-    for u in range(parts, units):
-        if u + 2 < units:
-            for j in others:
-                a2a(u, j).wait_send()
-                a2a(u + 2, j).start()
-        project_and_share(u, current)
+    stages = [lambda u: project(u, current), join_mate, join_across, join_all]
+    for turn in range(2 * (parts - 1) + len(stages)):
+        for i, u in reversed(list(enumerate(later))):
+            if 0 <= turn - 2 * i < len(stages):
+                stages[turn - 2 * i](u)
     for j in others:
         from_all(losses, loss_send, loss_recv, j)
     loss = losses[0]
@@ -397,8 +426,7 @@
 
     for j in others:
         for u in range(parts, units):
-            if u + 2 >= units:
-                a2a(u, j).wait_send()
+            a2a(u, j).wait_send()
         to_all(counts, count_send, count_recv, j).wait_send()
         to_all(losses, loss_send, loss_recv, j).wait_send()
         if not paired:
@@ -485,7 +513,7 @@
             pltpu.VMEM((rows, width), BF16),
             pltpu.VMEM((rows, width), BF16),
             pltpu.VMEM((rows, width), BF16),
-            pltpu.VMEM((together, width), F32),
+            pltpu.VMEM((units, together, width), F32),
             pltpu.VMEM((units, together, width), BF16),
             pltpu.VMEM((units, together, width), BF16),
             pltpu.VMEM((n, 8, LANES), F32),

time: 106 us -> 86.6 us (0.82)
  Pallas kernels: 105 us -> 85.2 us
    pallas_call x1, Pallas kernels: 100 us -> 80.8 us  [body(): pl.pallas_call(functools.partial(window_kernel, n, replicas, dims), out_s...]
where the time goes in v5:
time: 86.6 us; the launch traced here: 86.5 us
  Pallas kernels  85.2 us (98%)
  between operations  1.29 us (1%)
    pallas_call x1, Pallas kernels, body(): pl.pallas_call(functools.partial(window_kernel, n, replicas, dims), out_s...  80.8 us
    pallas_call x1, Pallas kernels, body(): pl.pallas_call(functools.partial(finish_kernel, model ** (-0.5), fw), out...  4.42 us

profile of v5, /device:TPU:0, one launch (start us, length us, event | category | flops | bytes accessed | tf_op | source)
XLA Modules:
  0.0 86.5 jit_solution(13530427097285827125)
XLA Ops:
  1.3 80.8 %window.1 = (f32[2048,512]{1,0:T(8,128)S(1)}, f32[2048,512]{1,0:T(8,128)S(1)}, f32[2048,512]{1,0:T(8,128)S(1)}, bf16[2,2048,256]{2,1,0:T(8,128)(2,1)S(1)}, bf16[...) custom-call(bf16[1,2,64,8192]{3,2,1,0:T(8,128)(2,1)} %hidden.1, bf16[1,2,64,512]{3,2,1,0:T(8,128)(2,1)} %targets_in.1, ...), custom_call_target="tpu_custom_call" | custom-call | tf_op jit(solution)/shard_map/window/pallas_call | solution.py:498
  82.0 4.4 %finish.1 = (f32[1,2048,512]{2,1,0:T(8,128)}, f32[1,2]{1,0:T(1,128)}) custom-call(s32[1]{0:T(128)S(6)} %copy.11.fragment, f32[2048,512]{1,0:T(8,128)S(1)} %get-tuple-element.8.kept, f32[2048,512]{1,0:T(8,128)S(1)} %get-tuple-element.9.first, f32[2048,512]{1,0:T(8,128)S(1)} %get-tuple-element.10.second, bf16[2,2048,256]{2,1,0:T(8,128)(2,1)S(1)} %get-tuple-element.11.turned, ...), custom_call_target="tpu_custom_call" | custom-call | tf_op jit(solution)/shard_map/finish/pallas_call | solution.py:545

commit v6 on v5

--- a/solution.py
+++ b/solution.py
@@ -26,7 +26,7 @@
 def adam_update(master, first, second, gradient):
     first = BETA_FIRST * first + (1.0 - BETA_FIRST) * gradient
     second = BETA_SECOND * second + (1.0 - BETA_SECOND) * gradient * gradient
-    master = master - INNER_RATE * (first / (jnp.sqrt(second) + ADAM_EPS) + DECAY_RATE * master)
+    master = master - INNER_RATE * (first / (second * lax.rsqrt(second) + ADAM_EPS) + DECAY_RATE * master)
     return (master, first, second)
 
 
@@ -90,29 +90,6 @@
     for copy in local:
         copy.start()
 
-    barrier = pltpu.get_barrier_semaphore()
-    for j in others:
-        pl.semaphore_signal(barrier, inc=1, device_id=(rep, j), device_id_type=MESH)
-    for i in peers:
-        pl.semaphore_signal(barrier, inc=1, device_id=(i, me), device_id_type=MESH)
-    pl.semaphore_wait(barrier, n + replicas - 2)
-
-    def a2a(u, j):
-        return pltpu.make_async_remote_copy(
-            src_ref=held_tokens(u, j), dst_ref=cols.at[u, my_tokens, :],
-            send_sem=a2a_send.at[u, j], recv_sem=a2a_recv.at[u, me],
-            device_id=(rep, j), device_id_type=MESH)
-
-    def a2a_arrived(u, j):
-        pltpu.make_async_remote_copy(
-            src_ref=held_tokens(u, j), dst_ref=cols.at[u, block(slot(j), few), :],
-            send_sem=a2a_send.at[u, j], recv_sem=a2a_recv.at[u, j],
-            device_id=(rep, j), device_id_type=MESH).wait_recv()
-
-    for u in range(parts):
-        for j in others:
-            a2a(u, j).start()
-
     local[7 + units].wait()
     lane = lax.broadcasted_iota(jnp.int32, (tokens, LANES), 1).astype(F32)
     eye = (lax.broadcasted_iota(jnp.int32, (tokens, tokens), 0)
@@ -130,6 +107,13 @@
         tally = tally + jnp.where(row8 == s, jnp.sum(onehot, axis=0, keepdims=True), 0.0)
     counts[me] = tally
 
+    barrier = pltpu.get_barrier_semaphore()
+    for j in others:
+        pl.semaphore_signal(barrier, inc=1, device_id=(rep, j), device_id_type=MESH)
+    for i in peers:
+        pl.semaphore_signal(barrier, inc=1, device_id=(i, me), device_id_type=MESH)
+    pl.semaphore_wait(barrier, n + replicas - 2)
+
     def to_all(buf, send, recv, j):
         return pltpu.make_async_remote_copy(
             src_ref=buf.at[me], dst_ref=buf.at[me], send_sem=send.at[j], recv_sem=recv.at[me],
@@ -142,6 +126,23 @@
 
     for j in others:
         to_all(counts, count_send, count_recv, j).start()
+
+    def a2a(u, j):
+        return pltpu.make_async_remote_copy(
+            src_ref=held_tokens(u, j), dst_ref=cols.at[u, my_tokens, :],
+            send_sem=a2a_send.at[u, j], recv_sem=a2a_recv.at[u, me],
+            device_id=(rep, j), device_id_type=MESH)
+
+    def a2a_arrived(u, j):
+        pltpu.make_async_remote_copy(
+            src_ref=held_tokens(u, j), dst_ref=cols.at[u, block(slot(j), few), :],
+            send_sem=a2a_send.at[u, j], recv_sem=a2a_recv.at[u, j],
+            device_id=(rep, j), device_id_type=MESH).wait_recv()
+
+    for u in range(parts):
+        for j in others:
+            a2a(u, j).start()
+
 
     local[0].wait()
     picked = fragment[0]
@@ -196,37 +197,7 @@
         coef_mine[...] = lines
         across().start()
 
-    for i in peers:
-        pltpu.make_async_remote_copy(
-            src_ref=frag_recv.at[i], dst_ref=frag_recv.at[i], send_sem=frag_send.at[i],
-            recv_sem=frag_got.at[i], device_id=(i, me), device_id_type=MESH).wait_recv()
-    local[2].wait()
-    local[3].wait()
-    base = anchor_ref[...].astype(F32)
-    delta = base - frag_recv[0].astype(F32)
-    for i in range(1, replicas):
-        delta = delta + (base - frag_recv[i].astype(F32))
-    mean_delta = delta / replicas
-    new_moment = NESTEROV * moment_ref[...].astype(F32) + mean_delta
-    frag_all[my_frag, :] = base - OUTER_RATE * (mean_delta + NESTEROV * new_moment)
-
-    def all_copy(i):
-        return pltpu.make_async_remote_copy(
-            src_ref=frag_all.at[my_frag, :], dst_ref=frag_all.at[my_frag, :],
-            send_sem=all_send.at[i], recv_sem=all_got.at[rep],
-            device_id=(i, me), device_id_type=MESH)
-
-    for i in peers:
-        all_copy(i).start()
-
     local[6 + units].wait()
-
-    if paired:
-        across().wait_recv()
-        for s in range(steps):
-            line = jnp.broadcast_to(coef_got[s:s + 1, :], (tokens, LANES))
-            column = jnp.sum(jnp.where(wide_eye, line, 0.0), axis=1, keepdims=True)
-            coef_across[s] = jnp.broadcast_to(column, (tokens, LANES))
 
     def part_copy(u, j):
         return pltpu.make_async_remote_copy(
@@ -372,15 +343,46 @@
 
     now, later = range(parts), range(parts, units)
     queue = [(u, j) for u in later for j in others]
-    for j in others:
-        for u in now:
+    project(0, w_ref)
+    for u in now:
+        for j in others:
             a2a(u, j).wait_send()
     a2a(*queue[0]).start()
-    for u in now:
+    for u in now[1:]:
         project(u, w_ref)
+    if paired:
+        across().wait_recv()
+        for s in range(steps):
+            line = jnp.broadcast_to(coef_got[s:s + 1, :], (tokens, LANES))
+            column = jnp.sum(jnp.where(wide_eye, line, 0.0), axis=1, keepdims=True)
+            coef_across[s] = jnp.broadcast_to(column, (tokens, LANES))
     for u in now:
         join_mate(u)
     a2a(*queue[1]).start()
+
+    for i in peers:
+        pltpu.make_async_remote_copy(
+            src_ref=frag_recv.at[i], dst_ref=frag_recv.at[i], send_sem=frag_send.at[i],
+            recv_sem=frag_got.at[i], device_id=(i, me), device_id_type=MESH).wait_recv()
+    local[2].wait()
+    local[3].wait()
+    base = anchor_ref[...].astype(F32)
+    delta = base - frag_recv[0].astype(F32)
+    for i in range(1, replicas):
+        delta = delta + (base - frag_recv[i].astype(F32))
+    mean_delta = delta / replicas
+    new_moment = NESTEROV * moment_ref[...].astype(F32) + mean_delta
+    frag_all[my_frag, :] = base - OUTER_RATE * (mean_delta + NESTEROV * new_moment)
+
+    def all_copy(i):
+        return pltpu.make_async_remote_copy(
+            src_ref=frag_all.at[my_frag, :], dst_ref=frag_all.at[my_frag, :],
+            send_sem=all_send.at[i], recv_sem=all_got.at[rep],
+            device_id=(i, me), device_id_type=MESH)
+
+    for i in peers:
+        all_copy(i).start()
+
     for u in now:
         join_across(u)
     for u, j in queue[2:]:
@@ -391,12 +393,6 @@
     local[5].wait()
     rt = 128
 
-    for i in peers:
-        at = block(i, own)
-        pltpu.make_async_remote_copy(
-            src_ref=frag_all.at[at, :], dst_ref=frag_all.at[at, :], send_sem=all_send.at[i],
-            recv_sem=all_got.at[i], device_id=(i, me), device_id_type=MESH).wait_recv()
-
     @pl.loop(0, rows // rt)
     def _(c):
         at = block(c, rt)
@@ -406,17 +402,31 @@
         current[at, :] = new_master.astype(BF16)
         first[at, :] = (INNER_RATE * BETA_FIRST) * new_first
         second[at, :] = BETA_SECOND * new_second
-        kept = (1.0 - INNER_RATE * DECAY_RATE) * new_master
-        mixed = (1.0 - MIXING) * frag_all[at, :]
-        for k in range(width // fw):
-            piece = kept[:, k * fw:(k + 1) * fw]
-            master[at, k * fw:(k + 1) * fw] = jnp.where(picked == k, MIXING * piece + mixed, piece)
+        master[at, :] = (1.0 - INNER_RATE * DECAY_RATE) * new_master
+
+    def mix():
+        for i in peers:
+            at = block(i, own)
+            pltpu.make_async_remote_copy(
+                src_ref=frag_all.at[at, :], dst_ref=frag_all.at[at, :], send_sem=all_send.at[i],
+                recv_sem=all_got.at[i], device_id=(i, me), device_id_type=MESH).wait_recv()
+
+        @pl.loop(0, rows // rt)
+        def _(c):
+            at = block(c, rt)
+            mixed = (1.0 - MIXING) * frag_all[at, :]
+            for k in range(width // fw):
+                piece = master[at, k * fw:(k + 1) * fw]
+                master[at, k * fw:(k + 1) * fw] = jnp.where(
+                    picked == k, MIXING * piece + mixed, piece)
 
     stages = [lambda u: project(u, current), join_mate, join_across, join_all]
     for turn in range(2 * (parts - 1) + len(stages)):
         for i, u in reversed(list(enumerate(later))):
             if 0 <= turn - 2 * i < len(stages):
                 stages[turn - 2 * i](u)
+        if turn == 0:
+            mix()
     for j in others:
         from_all(losses, loss_send, loss_recv, j)
     loss = losses[0]

time: 86.6 us -> 84.4 us (0.975)
  Pallas kernels: 85.2 us -> 82.9 us
    pallas_call x1, Pallas kernels: 80.8 us -> 78.5 us  [body(): pl.pallas_call(functools.partial(window_kernel, n, replicas, dims), out_s...]
where the time goes in v6:
time: 84.4 us; the launch traced here: 84.2 us
  Pallas kernels  82.9 us (98%)
  between operations  1.29 us (2%)
    pallas_call x1, Pallas kernels, body(): pl.pallas_call(functools.partial(window_kernel, n, replicas, dims), out_s...  78.5 us
    pallas_call x1, Pallas kernels, body(): pl.pallas_call(functools.partial(finish_kernel, model ** (-0.5), fw), out...  4.42 us

profile of v6, /device:TPU:0, one launch (start us, length us, event | category | flops | bytes accessed | tf_op | source)
XLA Modules:
  0.0 84.2 jit_solution(11455160209942342877)
XLA Ops:
  1.3 78.5 %window.1 = (f32[2048,512]{1,0:T(8,128)S(1)}, f32[2048,512]{1,0:T(8,128)S(1)}, f32[2048,512]{1,0:T(8,128)S(1)}, bf16[2,2048,256]{2,1,0:T(8,128)(2,1)S(1)}, bf16[...) custom-call(bf16[1,2,64,8192]{3,2,1,0:T(8,128)(2,1)} %hidden.1, bf16[1,2,64,512]{3,2,1,0:T(8,128)(2,1)} %targets_in.1, ...), custom_call_target="tpu_custom_call" | custom-call | tf_op jit(solution)/shard_map/window/pallas_call | solution.py:508
  79.8 4.4 %finish.1 = (f32[1,2048,512]{2,1,0:T(8,128)}, f32[1,2]{1,0:T(1,128)}) custom-call(s32[1]{0:T(128)S(6)} %copy.11.fragment, f32[2048,512]{1,0:T(8,128)S(1)} %get-tuple-element.8.kept, f32[2048,512]{1,0:T(8,128)S(1)} %get-tuple-element.9.first, f32[2048,512]{1,0:T(8,128)S(1)} %get-tuple-element.10.second, bf16[2,2048,256]{2,1,0:T(8,128)(2,1)S(1)} %get-tuple-element.11.turned, ...), custom_call_target="tpu_custom_call" | custom-call | tf_op jit(solution)/shard_map/finish/pallas_call | solution.py:555

commit v7 on v6

--- a/solution.py
+++ b/solution.py
@@ -344,9 +344,7 @@
     now, later = range(parts), range(parts, units)
     queue = [(u, j) for u in later for j in others]
     project(0, w_ref)
-    for u in now:
-        for j in others:
-            a2a(u, j).wait_send()
+    a2a(now[-1], others[0]).wait_send()
     a2a(*queue[0]).start()
     for u in now[1:]:
         project(u, w_ref)
@@ -434,9 +432,10 @@
         loss = loss + losses[j]
     loss_out[...] = loss
 
-    for j in others:
-        for u in range(parts, units):
-            a2a(u, j).wait_send()
+    for k, j in enumerate(others):
+        for u in range(units):
+            if (u, k) != (parts - 1, 0):
+                a2a(u, j).wait_send()
         to_all(counts, count_send, count_recv, j).wait_send()
         to_all(losses, loss_send, loss_recv, j).wait_send()
         if not paired:

time: 84.4 us -> 85.5 us (1.013)
  Pallas kernels: 82.9 us -> 84.1 us
    pallas_call x1, Pallas kernels: 78.5 us -> 79.6 us  [body(): pl.pallas_call(functools.partial(window_kernel, n, replicas, dims), out_s...]
where the time goes in v7:
time: 85.5 us; the launch traced here: 85.4 us
  Pallas kernels  84.1 us (98%)
  between operations  1.29 us (2%)
    pallas_call x1, Pallas kernels, body(): pl.pallas_call(functools.partial(window_kernel, n, replicas, dims), out_s...  79.6 us
    pallas_call x1, Pallas kernels, body(): pl.pallas_call(functools.partial(finish_kernel, model ** (-0.5), fw), out...  4.42 us

profile of v7, /device:TPU:0, one launch (start us, length us, event | category | flops | bytes accessed | tf_op | source)
XLA Modules:
  0.0 85.4 jit_solution(1055326310716738979)
XLA Ops:
  1.3 79.6 %window.1 = (f32[2048,512]{1,0:T(8,128)S(1)}, f32[2048,512]{1,0:T(8,128)S(1)}, f32[2048,512]{1,0:T(8,128)S(1)}, bf16[2,2048,256]{2,1,0:T(8,128)(2,1)S(1)}, bf16[...) custom-call(bf16[1,2,64,8192]{3,2,1,0:T(8,128)(2,1)} %hidden.1, bf16[1,2,64,512]{3,2,1,0:T(8,128)(2,1)} %targets_in.1, ...), custom_call_target="tpu_custom_call" | custom-call | tf_op jit(solution)/shard_map/window/pallas_call | solution.py:507
  80.9 4.4 %finish.1 = (f32[1,2048,512]{2,1,0:T(8,128)}, f32[1,2]{1,0:T(1,128)}) custom-call(s32[1]{0:T(128)S(6)} %copy.11.fragment, f32[2048,512]{1,0:T(8,128)S(1)} %get-tuple-element.8.kept, f32[2048,512]{1,0:T(8,128)S(1)} %get-tuple-element.9.first, f32[2048,512]{1,0:T(8,128)S(1)} %get-tuple-element.10.second, bf16[2,2048,256]{2,1,0:T(8,128)(2,1)S(1)} %get-tuple-element.11.turned, ...), custom_call_target="tpu_custom_call" | custom-call | tf_op jit(solution)/shard_map/finish/pallas_call | solution.py:554
